TPU v7x, 256 devices: a whole 4x4x8 slice. The times are simulated.
256 devices in a mesh: load: 8 (over x, y_lo), gz: 32 (over z, y_hi, core).
Axes of the slice: x: 4, y: 4 (y_hi: 2, y_lo: 2; y = y_hi * 2 + y_lo), z: 8, core: 2. Of those that a mesh axis runs over, the one named last changes fastest.
Arguments:
- density: float32 [64, 64, 128], P('gz', 'load'), may hold values from 0.1 to 1
- labels: int32 [64, 64, 128], P('gz'), may hold values from 0 to 11
- forces: float32 [16, 3, 64, 64, 128], P('load', None, 'gz'), may hold values from -6 to 6
- case_weights: int32 [16], replicated, may hold values from 1 to 4
Outputs:
- new_density: float32 [64, 64, 128], P('gz', 'load')
- displacement: float32 [16, 3, 64, 64, 128], P('load', None, 'gz')
All inputs are finite; a program needn't handle non-finite values.
Results may differ from a plain program's by a relative error of at most 0.00016.
Values sent between devices are 32-bit elements; how exact they have to be, the bound alone decides.
A program may use at most 64 MiB of HBM per device.

v0:
```python
import functools

import jax
import jax.numpy as jnp
import numpy as np
from jax import lax
from jax.experimental import pallas as pl
from jax.experimental.pallas import tpu as pltpu
from jax.sharding import PartitionSpec as P

MESH = pl.DeviceIdType.MESH
SWEEPS = 3
EMIN = 0.001
LOWER_EIG = 0.1
UPPER_EIG = 2.5
MOVE_LIMIT = 0.2
FLOOR_DENSITY = 0.001
THETA = 0.5 * (UPPER_EIG + LOWER_EIG)
DELTA = 0.5 * (UPPER_EIG - LOWER_EIG)
POISSON = 0.3
SHEAR = 1.0 / (2 * (1 + POISSON))
RATIO = 2 * POISSON / (1 - 2 * POISSON)
UNIT = SHEAR / 16.0
DIAG = UNIT * ((RATIO + 4.0) + (2.0 * (RATIO + 3.0) + 2.0) / 3.0 + (RATIO + 4.0) / 9.0)
EDGE = 1.5 - float(np.sqrt(2.0))


def chebyshev():
    sigma = THETA / DELTA
    factor = 1.0 / sigma
    pairs = []
    for _ in range(SWEEPS):
        following = 1.0 / (2.0 * sigma - factor)
        pairs.append((following * factor, 2.0 * following / DELTA))
        factor = following
    return pairs


def kernel(
    NL, Z, density, labels, forces, weights, newd, disp,
    F, LAB, D, DOWN, LNAT, EM, TX, INVD, R, STEP, SOL, XA, XD, UP, GU, OUT,
    PA, PB, V, G, QN, MS, RX, DS, SV, RX2,
    s_load, r_load, s_f, r_f, s_l, r_l, s_d, r_d, s_gh, r_gh, s_x, r_x, s_o, r_o, s_m, r_m, s_h, r_h, s_s, r_s, loc,
):
    rows = 8 * NL
    f32 = jnp.float32
    l = lax.axis_index("load")
    g = lax.axis_index("gz")
    core = g % 2
    yh = (g // 2) % 2
    z = g // 4

    def dev(ll, zz, yy, cc):
        return (lax.rem(ll + NL, NL), (lax.rem(zz + Z, Z) * 2 + yy) * 2 + cc)

    def remote(src, dst, ssem, rsem, target):
        return pltpu.make_async_remote_copy(
            src_ref=src, dst_ref=dst, send_sem=ssem, recv_sem=rsem, device_id=target, device_id_type=MESH
        )

    def arrived(ref, sem):
        pltpu.make_async_copy(ref, ref, sem).wait()

    lane = lax.broadcasted_iota(jnp.int32, (8, 128), 1)

    def xnext(v):
        return jnp.where(lane == 127, 0.0, pltpu.roll(v, 127, 1))

    def xprev(v):
        return jnp.where(lane == 0, 0.0, pltpu.roll(v, 1, 1))

    barrier = pltpu.get_barrier_semaphore()

    def greet(target):
        pl.semaphore_signal(barrier, inc=1, device_id=target, device_id_type=MESH)

    for a, b in ((0, 1), (1, 0), (1, 1)):
        greet(dev(l, z, (yh + a) % 2, (core + b) % 2))
    for k in range(1, NL):
        greet(dev(l + k, z, yh, core))
    for cc in range(2):
        greet(dev(l, z + 2 * core - 1, 1 - core, cc))
    for k in range(1, Z):
        greet(dev(l, z + k, yh, core))

    own_labels = pltpu.make_async_copy(labels, LNAT, loc.at[0])
    own_labels.start()
    zero8 = jnp.zeros((8, 128), f32)
    for r in range(12):
        D[r, 0:8, :] = zero8
        D[r, rows + 8 : rows + 16, :] = zero8
    for r in range(8):
        V[r, 0:8, :] = zero8
        V[r, rows + 8 : rows + 16, :] = zero8
    for m in range(9):
        TX[m, 0:8, :] = zero8
    for f in range(6):
        GU[f, 0:8, :] = zero8
    for k in range(2):
        QN[k, 0:8, :] = zero8
        QN[k, rows + 8 : rows + 16, :] = zero8
        for c in range(3):
            for m in range(10):
                XA[k, c, m, rows : rows + 8, :] = zero8
                XD[k, c, m, rows : rows + 8, :] = zero8
    for k in range(4):
        for t in range(3):
            DS[k, 8 * t : 8 * t + 8, :] = zero8
    for c in range(NL):
        for k in range(4):
            MS[c, k, 8:16, :] = zero8
    pl.semaphore_wait(barrier, 3 + (NL - 1) + 2 + (Z - 1))

    mine = pl.ds(pl.multiple_of(8 * l, 8), 8)
    load_copies = []
    for k in range(1, NL):
        cp = remote(density, DOWN.at[:, mine, :], s_load.at[k - 1], r_load, dev(l + k, z, yh, core))
        cp.start()
        load_copies.append(cp)
    load_self = pltpu.make_async_copy(density, DOWN.at[:, mine, :], r_load)
    load_self.start()

    first = (1 - yh) * 4 + 2 * core
    slot = first // 2
    zn = z + 2 * yh - 1
    targets = [(z, 0, yh), (z, 1, yh), (zn, 0, 1 - yh), (zn, 1, 1 - yh)]
    is_self = [jnp.logical_and(yh == 0, core == 0), jnp.logical_and(yh == 1, core == 1)]
    own_core = [yh, yh, 1 - yh, 1 - yh]

    def spread(make, local):
        for t, (zz, yy, cc) in enumerate(targets):
            if t < 2:
                @pl.when(is_self[t])
                def _():
                    local(t).start()

                @pl.when(jnp.logical_not(is_self[t]))
                def _():
                    make(t, dev(l, zz, yy, cc)).start()
            else:
                make(t, dev(l, zz, yy, cc)).start()

    def spread_sent(make):
        for t, (zz, yy, cc) in enumerate(targets):
            if t < 2:
                @pl.when(jnp.logical_not(is_self[t]))
                def _():
                    make(t, dev(l, zz, yy, cc)).wait_send()
            else:
                make(t, dev(l, zz, yy, cc)).wait_send()

    def f_dst():
        return F.at[:, pl.ds(first, 2), :, :]

    def f_make(t, target):
        return remote(forces.at[t % 2], f_dst(), s_f.at[t], r_f.at[slot], target)

    def f_local(t):
        return pltpu.make_async_copy(forces.at[t % 2], f_dst(), r_f.at[slot])

    def l_make(t, target):
        return remote(labels, LAB.at[pl.ds(first + 4 * own_core[t], 2)], s_l.at[t], r_l.at[slot + 2 * own_core[t]], target)

    def l_local(t):
        return pltpu.make_async_copy(labels, LAB.at[pl.ds(first + 4 * own_core[t], 2)], r_l.at[slot + 2 * own_core[t]])

    def d_dst(t):
        return D.at[pl.ds(first + 4 * own_core[t], 2), 8 : rows + 8, :]

    def d_make(t, target):
        return remote(DOWN, d_dst(t), s_d.at[t], r_d.at[slot + 2 * own_core[t]], target)

    def d_local(t):
        return pltpu.make_async_copy(DOWN, d_dst(t), r_d.at[slot + 2 * own_core[t]])

    is_a1 = jnp.logical_and(yh == 0, core == 1)

    def le_make():
        return remote(labels, LAB.at[2:4], s_l.at[4], r_l.at[1], dev(l, z, 1, 1))

    def de_make():
        return remote(DOWN, D.at[2:4, 8 : rows + 8, :], s_d.at[4], r_d.at[1], dev(l, z, 1, 1))

    spread(f_make, f_local)
    spread(l_make, l_local)

    @pl.when(is_a1)
    def _():
        le_make().start()
        pltpu.make_async_copy(labels, LAB.at[2:4], r_l.at[1]).start()

    arrived(DOWN, r_load)
    spread(d_make, d_local)

    @pl.when(is_a1)
    def _():
        de_make().start()
        pltpu.make_async_copy(DOWN, D.at[2:4, 8 : rows + 8, :], r_d.at[1]).start()

    own_labels.wait()
    for k in range(2):
        for c in range(NL):
            d = DOWN[k, 8 * c : 8 * c + 8, :]
            solid = jnp.where(LNAT[k, 8 * c : 8 * c + 8, :] == 2, 1.0, d)
            QN[k, 8 * c + 8 : 8 * c + 16, :] = d * solid * solid

    for k in range(4):
        at = 2 * k + 4 * core
        arrived(LAB.at[pl.ds(at, 2)], r_l.at[k + 2 * core])
        arrived(D.at[pl.ds(at, 2), 8 : rows + 8, :], r_d.at[k + 2 * core])

    @pl.when(core == 1)
    def _():
        arrived(LAB.at[2:4], r_l.at[1])
        arrived(D.at[2:4, 8 : rows + 8, :], r_d.at[1])

    sibling = dev(l, z, yh, 1 - core)

    def up_make():
        return remote(D.at[4:6, 8 : rows + 8, :], D.at[0:2, 8 : rows + 8, :], s_gh, r_gh, sibling)

    def down_make():
        return remote(D.at[4:8, 8 : rows + 8, :], D.at[8:12, 8 : rows + 8, :], s_gh, r_gh, sibling)

    @pl.when(core == 0)
    def _():
        up_make().start()

    @pl.when(core == 1)
    def _():
        down_make().start()

    sgn = 2 * core - 1

    def inside(p):
        at = 8 * z + p
        return jnp.logical_and(at >= 0, at < 8 * Z)

    def moduli_layer(m, _):
        p = 3 + sgn * m
        r = p + 4 * (1 - core)
        scale = jnp.where(inside(p), f32(UNIT), f32(0.0))
        for c in range(NL):
            d = D[r, 8 * c + 8 : 8 * c + 16, :]
            solid = jnp.where(LAB[r, 8 * c : 8 * c + 8, :] == 2, 1.0, d)
            e = (EMIN + (1.0 - EMIN) * solid * solid * solid) * scale
            EM[m, 8 * c : 8 * c + 8, :] = e
            TX[m, 8 * c + 8 : 8 * c + 16, :] = e + xprev(e)
        return 0

    lax.fori_loop(0, 8 + core, moduli_layer, 0)
    nodes = 7 + core

    def inverse_layer(m, _):
        p = jnp.where(core == 1, 3 + m, 4 - m)
        r = p + 4 * (1 - core)
        keep = inside(p).astype(jnp.int32)
        for c in range(NL):
            near = TX[m, 8 * c + 8 : 8 * c + 16, :] + TX[m, 8 * c + 7 : 8 * c + 15, :]
            far = TX[m - 1, 8 * c + 8 : 8 * c + 16, :] + TX[m - 1, 8 * c + 7 : 8 * c + 15, :]
            lab = LAB[r, 8 * c : 8 * c + 8, :] * keep + (1 - keep)
            INVD[m, 8 * c : 8 * c + 8, :] = jnp.where(lab != 1, (UNIT / DIAG) / (near + far), 0.0)
        return 0

    lax.fori_loop(1, nodes + 1, inverse_layer, 0)

    @pl.when(core == 0)
    def _():
        arrived(D.at[8:12, 8 : rows + 8, :], r_gh)

    @pl.when(core == 1)
    def _():
        arrived(D.at[0:2, 8 : rows + 8, :], r_gh)

    def plane_sums(center, above, below):
        ysum = above + below
        xsum = xnext(center) + xprev(center)
        cross = ysum + xsum
        corner = xnext(ysum) + xprev(ysum)
        return 1.5 * center + 0.5 * cross + EDGE * corner, 0.5 * center + EDGE * cross

    def d_plane(r, _):
        p = r - 4 * (1 - core)
        scale = jnp.where(inside(p), f32(1.0), f32(0.0))
        for c in range(NL):
            a, b = plane_sums(
                D[r, 8 * c + 8 : 8 * c + 16, :], D[r, 8 * c + 7 : 8 * c + 15, :], D[r, 8 * c + 9 : 8 * c + 17, :]
            )
            PA[r, 8 * c : 8 * c + 8, :] = a * scale
            PB[r, 8 * c : 8 * c + 8, :] = b * scale
        return 0

    lax.fori_loop(1, 11, d_plane, 0)

    def v_plane(r, _):
        p = r - 4 * (1 - core)
        ok = jnp.where(inside(p), f32(1.0), f32(0.0))
        for c in range(NL):
            at = slice(8 * c, 8 * c + 8)
            total = PA[r, at, :] + PB[r - 1, at, :] + PB[r + 1, at, :]
            V[r - 2, 8 * c + 8 : 8 * c + 16, :] = ok / (total + (1.0 - ok))
        return 0

    lax.fori_loop(2, 10, v_plane, 0)

    def w_plane(r, _):
        for c in range(NL):
            a, b = plane_sums(
                V[r - 2, 8 * c + 8 : 8 * c + 16, :], V[r - 2, 8 * c + 7 : 8 * c + 15, :], V[r - 2, 8 * c + 9 : 8 * c + 17, :]
            )
            PA[r, 8 * c : 8 * c + 8, :] = a
            PB[r, 8 * c : 8 * c + 8, :] = b
        return 0

    lax.fori_loop(3, 9, w_plane, 0)

    def g_plane(k, _):
        r = k + 4
        for c in range(NL):
            at = slice(8 * c, 8 * c + 8)
            d = D[r, 8 * c + 8 : 8 * c + 16, :]
            solid = jnp.where(LAB[r, at, :] == 2, 1.0, d)
            G[k, at, :] = (PA[r, at, :] + PB[r - 1, at, :] + PB[r + 1, at, :]) * (d * solid * solid)
        return 0

    lax.fori_loop(0, 4, g_plane, 0)

    for k in range(4):
        arrived(F.at[:, 2 * k : 2 * k + 2, :, :], r_f.at[k])
    flip = jnp.where(core == 1, f32(1.0), f32(-1.0))

    def x_make(par):
        return [
            remote(X.at[par, :, 1, 0:rows, :], X.at[par, :, 0, 0:rows, :], s_x.at[par, n], r_x.at[par, n], sibling)
            for n, X in enumerate((XA, XD))
        ]

    def first_step(m, _):
        i = jnp.where(core == 1, m - 1, 8 - m)
        for c in range(NL):
            at = slice(8 * c, 8 * c + 8)
            inv = INVD[m, at, :]
            for comp in range(3):
                f = F[comp, i, at, :]
                if comp == 2:
                    f = f * flip
                R[comp, m, at, :] = f
                s = inv * f * (1.0 / THETA)
                STEP[comp, m, at, :] = s
                SOL[comp, m, at, :] = s
                n = xnext(s)
                XA[0, comp, m, at, :] = s + n
                XD[0, comp, m, at, :] = n - s

        @pl.when(m == 1)
        def _():
            for cp in x_make(0):
                cp.start()

        return 0

    lax.fori_loop(1, nodes + 1, first_step, 0)

    def fields(par, comp, m, c):
        a0 = XA[par, comp, m, 8 * c : 8 * c + 8, :]
        a1 = XA[par, comp, m, 8 * c + 1 : 8 * c + 9, :]
        d0 = XD[par, comp, m, 8 * c : 8 * c + 8, :]
        d1 = XD[par, comp, m, 8 * c + 1 : 8 * c + 9, :]
        return a0 + a1, a1 - a0, d0 + d1, d1 - d0

    def modes(par, m, c):
        out = []
        for comp in range(3):
            lo = fields(par, comp, m, c)
            hi = fields(par, comp, m + 1, c)
            out.append(
                dict(
                    z=hi[0] - lo[0], y=hi[1] + lo[1], yz=hi[1] - lo[1], x=hi[2] + lo[2], zx=hi[2] - lo[2],
                    xy=hi[3] + lo[3], xyz=hi[3] - lo[3],
                )
            )
        return out

    def ghost(par):
        for n, X in enumerate((XA, XD)):
            arrived(X.at[par, :, 0, 0:rows, :], r_x.at[par, n])
            for c in range(NL):
                X[par, 2, 0, 8 * c : 8 * c + 8, :] = -X[par, 2, 0, 8 * c : 8 * c + 8, :]

    coefs = chebyshev()

    def sweep(s, _):
        par = s % 2
        nxt = 1 - par
        c1, c2 = f32(coefs[0][0]), f32(coefs[0][1])
        for n in range(1, SWEEPS):
            c1 = jnp.where(s == n, f32(coefs[n][0]), c1)
            c2 = jnp.where(s == n, f32(coefs[n][1]), c2)
        last = jnp.where(s == SWEEPS - 1, f32(1.0), f32(0.0))
        count = nodes - 1 - s
        ghost(par)

        def layer(m, _):
            put = jnp.where(m == 0, 9, m)
            for c in range(NL):
                at = slice(8 * c, 8 * c + 8)
                u, v, w = modes(par, m, c)
                e = EM[m, at, :]
                e2, e3, eq = e + e, e * (1.0 / 3.0), e * ((RATIO + 4.0) / 9.0)
                tr = (0.5 * RATIO) * (u["x"] + v["y"] + w["z"])
                fx = e2 * (tr + u["x"])
                fy = e2 * (tr + v["y"])
                fz = e2 * (tr + w["z"])
                sxy = e * (u["y"] + v["x"])
                syz = e * (v["z"] + w["y"])
                szx = e * (u["z"] + w["x"])
                h = 0.5 * (v["xy"] + w["zx"])
                vxy, wzx = e * (v["xy"] + h), e * (w["zx"] + h)
                h = 0.5 * (u["xy"] + w["yz"])
                uxy, wyz = e * (u["xy"] + h), e * (w["yz"] + h)
                h = 0.5 * (u["zx"] + v["yz"])
                uzx, vyz = e * (u["zx"] + h), e * (v["yz"] + h)
                h = u["yz"] + v["zx"] + w["xy"]
                uyz, vzx, wxy = e3 * (u["yz"] + h), e3 * (v["zx"] + h), e3 * (w["xy"] + h)
                uq, vq, wq = eq * u["xyz"], eq * v["xyz"], eq * w["xyz"]
                forces_of = (
                    (szx, sxy, uyz, fx, uzx, uxy, uq),
                    (syz, fy, vyz, sxy, vzx, vxy, vq),
                    (fz, syz, wyz, szx, wzx, wxy, wq),
                )
                inv = INVD[m, at, :]
                for comp in range(3):
                    gz_, gy, gyz, gx, gzx, gxy, gxyz = forces_of[comp]
                    taa = UP[4 * comp, at, :] - gz_
                    tay = UP[4 * comp + 1, at, :] + (gy - gyz)
                    tda = UP[4 * comp + 2, at, :] + (gx - gzx)
                    tdy = UP[4 * comp + 3, at, :] + (gxy - gxyz)
                    UP[4 * comp, at, :] = gz_
                    UP[4 * comp + 1, at, :] = gy + gyz
                    UP[4 * comp + 2, at, :] = gx + gzx
                    UP[4 * comp + 3, at, :] = gxy + gxyz
                    GU[2 * comp, 8 * c + 8 : 8 * c + 16, :] = taa + tay
                    GU[2 * comp + 1, 8 * c + 8 : 8 * c + 16, :] = tda + tdy
                    a = (taa - tay) + GU[2 * comp, 8 * c + 7 : 8 * c + 15, :]
                    b = (tda - tdy) + GU[2 * comp + 1, 8 * c + 7 : 8 * c + 15, :]
                    pushed = (a - b) + xprev(a + b)
                    res = R[comp, m, at, :] - pushed
                    R[comp, put, at, :] = res
                    step = c1 * STEP[comp, m, at, :] + c2 * (inv * res)
                    STEP[comp, put, at, :] = step
                    before = SOL[comp, m, at, :]
                    SOL[comp, put, at, :] = before + step
                    sent = step + last * before
                    n = xnext(sent)
                    XA[nxt, comp, put, at, :] = sent + n
                    XD[nxt, comp, put, at, :] = n - sent

            @pl.when(m == 1)
            def _():
                for cp in x_make(par):
                    cp.wait_send()
                for cp in x_make(nxt):
                    cp.start()

            return 0

        lax.fori_loop(0, count + 1, layer, 0)
        return 0

    for f in range(12):
        for c in range(NL):
            UP[f, 8 * c : 8 * c + 8, :] = zero8
    for c in range(NL):
        at = slice(8 * c, 8 * c + 8)
        INVD[0, at, :] = zero8
        for comp in range(3):
            R[comp, 0, at, :] = zero8
            STEP[comp, 0, at, :] = zero8
            SOL[comp, 0, at, :] = zero8
    lax.fori_loop(0, SWEEPS, sweep, 0)

    def lay_out(k, _):
        m = jnp.where(core == 1, k + 1, 4 - k)
        for c in range(NL):
            at = slice(8 * c, 8 * c + 8)
            for comp in range(3):
                v = SOL[comp, m, at, :]
                OUT[comp, k, at, :] = v * flip if comp == 2 else v
        return 0

    lax.fori_loop(0, 4, lay_out, 0)

    fin = SWEEPS % 2
    ghost(fin)
    weight = weights[2 * l + yh].astype(f32)
    weight_sum = weights[0]
    for n in range(1, 2 * NL):
        weight_sum = weight_sum + weights[n]
    weight_sum = weight_sum.astype(f32)

    def energy_layer(k, share):
        m = jnp.where(core == 1, k + 1, 3 - k)
        for c in range(NL):
            u, v, w = modes(fin, m, c)
            tr = u["x"] + v["y"] + w["z"]
            sq = lambda t: t * t
            normal = sq(u["x"]) + sq(v["y"]) + sq(w["z"])
            shear = sq(u["y"] + v["x"]) + sq(v["z"] + w["y"]) + sq(u["z"] + w["x"])
            pairs = (
                sq(v["xy"]) + sq(w["zx"]) + sq(u["xy"]) + sq(w["yz"]) + sq(u["zx"]) + sq(v["yz"])
            )
            joint = sq(v["xy"] + w["zx"]) + sq(u["xy"] + w["yz"]) + sq(u["zx"] + v["yz"])
            s = u["yz"] + v["zx"] + w["xy"]
            triple = sq(u["yz"]) + sq(v["zx"]) + sq(w["xy"]) + sq(s)
            quad = sq(u["xyz"]) + sq(v["xyz"]) + sq(w["xyz"])
            total = (
                (RATIO * sq(tr) + 2.0 * normal + shear) + (pairs + 0.5 * joint)
                + (1.0 / 3.0) * triple + ((RATIO + 4.0) / 9.0) * quad
            )
            t = (weight * UNIT) * total
            MS[c, k, 0:8, :] = t
            if c > 0:
                MS[c - 1, k, 9:10, :] = t[0:1, :]
            if c < NL - 1:
                MS[c + 1, k, 8:9, :] = t[7:8, :]
            share = share + t * G[k, 8 * c : 8 * c + 8, :]
        return share

    share = lax.fori_loop(0, 4, energy_layer, zero8)
    share = jnp.sum(share, axis=0, keepdims=True)
    for c in range(NL):
        for k in (0, 2):
            MS[c, k, 10:11, :] = share

    me = 2 * l + yh
    m_copies = []
    both = yh == core

    def m_make(k, cc):
        ll = lax.rem(l + k, NL)
        return remote(MS.at[ll, 2 * cc : 2 * cc + 2], RX.at[me], s_m.at[k, cc], r_m, dev(ll, z, core, cc))

    for k in range(NL):
        for cc in range(2):
            if k > 0:
                m_make(k, cc).start()
            else:
                alone = jnp.logical_and(both, core == cc)

                @pl.when(alone)
                def _():
                    pltpu.make_async_copy(MS.at[l, 2 * cc : 2 * cc + 2], RX.at[me], r_m).start()

                @pl.when(jnp.logical_not(alone))
                def _():
                    m_make(k, cc).start()

    def o_make(cc):
        return remote(OUT.at[:, 2 * cc : 2 * cc + 2], disp.at[yh], s_o.at[cc], r_o.at[yh], dev(l, z, core, cc))

    for cc in range(2):
        alone = jnp.logical_and(both, core == cc)

        @pl.when(alone)
        def _():
            pltpu.make_async_copy(OUT.at[:, 2 * cc : 2 * cc + 2], disp.at[yh], r_o.at[yh]).start()

        @pl.when(jnp.logical_not(alone))
        def _():
            o_make(cc).start()

    arrived(RX, r_m)
    scale = (3.0 * (1.0 - EMIN)) / weight_sum
    mean_part = None
    sums = []
    for k in range(2):
        main, rim = RX[0, k, 0:8, :], RX[0, k, 8:16, :]
        for n in range(1, 2 * NL):
            main = main + RX[n, k, 0:8, :]
            rim = rim + RX[n, k, 8:16, :]
        sums.append((main, rim))
    SV[...] = sums[0][1][2:3, :]

    def s_make(kz, ky):
        return remote(SV, RX2.at[2 * z + yh], s_s.at[kz, ky], r_s, dev(l, z + kz, (yh + ky) % 2, core))

    for kz in range(Z):
        for ky in range(2):
            if (kz, ky) != (0, 0):
                s_make(kz, ky).start()
    pltpu.make_async_copy(SV, RX2.at[2 * z + yh], r_s).start()

    base = pl.multiple_of(8 * l, 8)
    for k in range(2):
        main, rim = sums[k]
        before = QN[k, pl.ds(base, 8), :]
        here = QN[k, pl.ds(base + 8, 8), :]
        after = QN[k, pl.ds(base + 16, 8), :]
        DS[k + 1, 8:16, :] = main * here * scale
        DS[k + 1, 7:8, :] = rim[0:1, :] * before[7:8, :] * scale
        DS[k + 1, 16:17, :] = rim[1:2, :] * after[0:1, :] * scale

    def h_make(up):
        to = lax.rem(g + (1 if up else 4 * Z - 1), 4 * Z)
        return remote(DS.at[2 if up else 1], DS.at[0 if up else 3], s_h.at[int(up)], r_h.at[int(up)], (l, to))

    for up in (False, True):
        h_make(up).start()
    arrived(DS.at[3], r_h.at[0])
    arrived(DS.at[0], r_h.at[1])

    planes = []
    for k in range(4):
        planes.append(plane_sums(DS[k, 8:16, :], DS[k, 7:15, :], DS[k, 9:17, :]))
    low = jnp.where(g > 0, f32(1.0), f32(0.0)) * planes[0][1]
    high = jnp.where(g < 4 * Z - 1, f32(1.0), f32(0.0)) * planes[3][1]
    numer = [planes[1][0] + low + planes[2][1], planes[2][0] + planes[1][1] + high]
    v_at = 4 * yh + 2 * (1 - core)
    arrived(RX2, r_s)
    total = RX2[0]
    for n in range(1, 2 * Z):
        total = total + RX2[n]
    mean = jnp.sum(total, axis=1, keepdims=True) * scale / (8 * Z * rows * 128)
    for k in range(2):
        filtered = numer[k] * V[v_at + k, pl.ds(base + 8, 8), :]
        d = DOWN[k, mine, :]
        candidate = d * jnp.sqrt(filtered / mean)
        lower = jnp.maximum(d - MOVE_LIMIT, FLOOR_DENSITY)
        upper = jnp.minimum(d + MOVE_LIMIT, 1.0)
        new = jnp.minimum(jnp.maximum(candidate, lower), upper)
        newd[k] = jnp.where(LNAT[k, mine, :] == 2, 1.0, new)

    for cp in load_copies:
        cp.wait_send()
    spread_sent(f_make)
    spread_sent(l_make)
    spread_sent(d_make)

    @pl.when(is_a1)
    def _():
        le_make().wait_send()
        de_make().wait_send()

    @pl.when(core == 0)
    def _():
        up_make().wait_send()

    @pl.when(core == 1)
    def _():
        down_make().wait_send()

    for cp in x_make(fin):
        cp.wait_send()
    for k in range(NL):
        for cc in range(2):
            if k > 0:
                m_make(k, cc).wait_send()
            else:
                @pl.when(jnp.logical_not(jnp.logical_and(both, core == cc)))
                def _():
                    m_make(k, cc).wait_send()
    for cc in range(2):
        @pl.when(jnp.logical_not(jnp.logical_and(both, core == cc)))
        def _():
            o_make(cc).wait_send()
    for kz in range(Z):
        for ky in range(2):
            if (kz, ky) != (0, 0):
                s_make(kz, ky).wait_send()
    for up in (False, True):
        h_make(up).wait_send()
    for k in range(2):
        arrived(disp.at[k], r_o.at[k])


def solution(mesh):
    NL, Z = mesh.shape["load"], mesh.shape["gz"] // 4
    rows = 8 * NL

    def on_device(density, labels, forces, case_weights):
        vm = lambda *shape: pltpu.VMEM(shape, jnp.float32)
        dma = lambda *shape: pltpu.SemaphoreType.DMA(shape)
        scratch = [
            vm(3, 8, rows, 128),
            pltpu.VMEM((12, rows, 128), jnp.int32),
            vm(12, rows + 16, 128),
            vm(2, rows, 128),
            pltpu.VMEM((2, rows, 128), jnp.int32),
            vm(9, rows, 128),
            vm(9, rows + 8, 128),
            vm(9, rows, 128),
            vm(3, 10, rows, 128),
            vm(3, 10, rows, 128),
            vm(3, 10, rows, 128),
            vm(2, 3, 10, rows + 8, 128),
            vm(2, 3, 10, rows + 8, 128),
            vm(12, rows, 128),
            vm(6, rows + 8, 128),
            vm(3, 4, rows, 128),
            vm(12, rows, 128),
            vm(12, rows, 128),
            vm(8, rows + 16, 128),
            vm(4, rows, 128),
            vm(2, rows + 16, 128),
            vm(NL, 4, 16, 128),
            vm(2 * NL, 2, 16, 128),
            vm(4, 24, 128),
            vm(1, 128),
            vm(2 * Z, 1, 128),
            dma(NL), pltpu.SemaphoreType.DMA,
            dma(4), dma(4),
            dma(5), dma(6),
            dma(5), dma(6),
            pltpu.SemaphoreType.DMA, pltpu.SemaphoreType.DMA,
            dma(2, 2), dma(2, 2),
            dma(2), dma(2),
            dma(NL, 2), pltpu.SemaphoreType.DMA,
            dma(2), dma(2),
            dma(Z, 2), pltpu.SemaphoreType.DMA,
            dma(1),
        ]
        return pl.pallas_call(
            functools.partial(kernel, NL, Z),
            out_shape=(
                jax.ShapeDtypeStruct(density.shape, jnp.float32),
                jax.ShapeDtypeStruct(forces.shape, jnp.float32),
            ),
            in_specs=[pl.BlockSpec(memory_space=pl.ANY)] * 3 + [pl.BlockSpec(memory_space=pltpu.SMEM)],
            out_specs=(pl.BlockSpec(memory_space=pltpu.VMEM), pl.BlockSpec(memory_space=pl.ANY)),
            scratch_shapes=scratch,
            compiler_params=pltpu.CompilerParams(
                collective_id=1, has_side_effects=True, vmem_limit_bytes=32 << 20
            ),
            name="step",
        )(density, labels, forces, case_weights)

    return jax.shard_map(
        on_device,
        mesh=mesh,
        in_specs=(
            P("gz", "load", None),
            P("gz", None, None),
            P("load", None, "gz", None, None),
            P(),
        ),
        out_specs=(P("gz", "load", None), P("load", None, "gz", None, None)),
        check_vma=False,
    )
```

profile of v0, /device:TPU:6, one launch (start us, length us, event | category | flops | bytes accessed | tf_op | source)
XLA Modules:
  0.0 83.3 jit_solution(7268163914078191400)
XLA Ops:
  0.6 0.0 copy-start
  0.6 1.0 %copy-done = f32[2,3,2,64,128]{4,3,2,1,0:T(8,128)S(1)} copy-done((f32[2,3,2,64,128]{4,3,2,1,0:T(8,128)S(1)}, f32[2,3,2,64,128]{4,3,2,1,0:T(8,128)}, u32[]{:S(2)}) %copy-start) | copy-done | bytes 393240
  1.6 0.0 copy-start.1
  1.6 0.8 %copy-done.1 = s32[2,64,128]{2,1,0:T(8,128)S(1)} copy-done((s32[2,64,128]{2,1,0:T(8,128)S(1)}, s32[2,64,128]{2,1,0:T(8,128)}, u32[]{:S(2)}) %copy-start.1) | copy-done | bytes 65560
  2.5 0.0 copy-start.2
  2.5 0.7 copy-done.2
  3.2 0.0 copy-start.3
  3.2 0.7 copy-done.3
  3.8 78.1 %step.1 = (f32[2,8,128]{2,1,0:T(8,128)S(1)}, f32[2,3,2,64,128]{4,3,2,1,0:T(8,128)S(1)}) custom-call(f32[2,8,128]{2,1,0:T(8,128)S(1)} %copy-done.2, s32[2,64,128]{2,1,0:T(8,128)S(1)} %copy-done.1, f32[2,3,2,64,128]{4,3,2,1,0:T(8,128)S(1)} %copy-done, s32[16]{0:T(128)S(1)} %copy-done.3), custom_call_target="tpu_custom_call" | custom-call | tf_op jit(solution)/shard_map/step/pallas_call | solution.py:722
  82.0 0.6 copy.8
  82.6 0.7 copy.9
Async XLA Ops:
  0.6 1.0 %copy-start = (f32[2,3,2,64,128]{4,3,2,1,0:T(8,128)S(1)}, f32[2,3,2,64,128]{4,3,2,1,0:T(8,128)}, u32[]{:S(2)}) copy-start(f32[2,3,2,64,128]{4,3,2,1,0:T(8,128)} %forces.1) | copy-start | bytes 1179652
  1.6 0.8 %copy-start.1 = (s32[2,64,128]{2,1,0:T(8,128)S(1)}, s32[2,64,128]{2,1,0:T(8,128)}, u32[]{:S(2)}) copy-start(s32[2,64,128]{2,1,0:T(8,128)} %labels.1) | copy-start | bytes 196612
  2.5 0.7 copy-start.2
  3.2 0.7 copy-start.3
where the time goes:
time: 83.5 us; the launch traced here: 83.3 us
  Pallas kernels  78.1 us (94%)
  local copies, waits for them, and re-layouts  4.53 us (5%)
    pallas_call x1, Pallas kernels, on_device(): pl.pallas_call(functools.partial(kernel, NL, Z), out_shape=(jax.ShapeDtyp...  78.1 us
    unnamed x10, local copies, waits for them, and re-layouts  4.53 us

commit v1 on v0

--- a/solution.py
+++ b/solution.py
@@ -38,12 +38,13 @@
 
 def kernel(
     NL, Z, density, labels, forces, weights, newd, disp,
-    F, LAB, D, DOWN, LNAT, EM, TX, INVD, R, STEP, SOL, XA, XD, UP, GU, OUT,
+    F, LAB, D, DOWN, LNAT, EM, TX, INVD, R, STEP, SOL, XA0, XA1, XD0, XD1, UP, GU, OUT,
     PA, PB, V, G, QN, MS, RX, DS, SV, RX2,
     s_load, r_load, s_f, r_f, s_l, r_l, s_d, r_d, s_gh, r_gh, s_x, r_x, s_o, r_o, s_m, r_m, s_h, r_h, s_s, r_s, loc,
 ):
     rows = 8 * NL
     f32 = jnp.float32
+    XA, XD = (XA0, XA1), (XD0, XD1)
     l = lax.axis_index("load")
     g = lax.axis_index("gz")
     core = g % 2
@@ -101,8 +102,8 @@
         QN[k, rows + 8 : rows + 16, :] = zero8
         for c in range(3):
             for m in range(10):
-                XA[k, c, m, rows : rows + 8, :] = zero8
-                XD[k, c, m, rows : rows + 8, :] = zero8
+                XA[k][c, m, rows : rows + 8, :] = zero8
+                XD[k][c, m, rows : rows + 8, :] = zero8
     for k in range(4):
         for t in range(3):
             DS[k, 8 * t : 8 * t + 8, :] = zero8
@@ -331,7 +332,7 @@
 
     def x_make(par):
         return [
-            remote(X.at[par, :, 1, 0:rows, :], X.at[par, :, 0, 0:rows, :], s_x.at[par, n], r_x.at[par, n], sibling)
+            remote(X[par].at[:, 1, 0:rows, :], X[par].at[:, 0, 0:rows, :], s_x.at[par, n], r_x.at[par, n], sibling)
             for n, X in enumerate((XA, XD))
         ]
 
@@ -349,8 +350,8 @@
                 STEP[comp, m, at, :] = s
                 SOL[comp, m, at, :] = s
                 n = xnext(s)
-                XA[0, comp, m, at, :] = s + n
-                XD[0, comp, m, at, :] = n - s
+                XA[0][comp, m, at, :] = s + n
+                XD[0][comp, m, at, :] = n - s
 
         @pl.when(m == 1)
         def _():
@@ -362,10 +363,10 @@
     lax.fori_loop(1, nodes + 1, first_step, 0)
 
     def fields(par, comp, m, c):
-        a0 = XA[par, comp, m, 8 * c : 8 * c + 8, :]
-        a1 = XA[par, comp, m, 8 * c + 1 : 8 * c + 9, :]
-        d0 = XD[par, comp, m, 8 * c : 8 * c + 8, :]
-        d1 = XD[par, comp, m, 8 * c + 1 : 8 * c + 9, :]
+        a0 = XA[par][comp, m, 8 * c : 8 * c + 8, :]
+        a1 = XA[par][comp, m, 8 * c + 1 : 8 * c + 9, :]
+        d0 = XD[par][comp, m, 8 * c : 8 * c + 8, :]
+        d1 = XD[par][comp, m, 8 * c + 1 : 8 * c + 9, :]
         return a0 + a1, a1 - a0, d0 + d1, d1 - d0
 
     def modes(par, m, c):
@@ -383,77 +384,82 @@
 
     def ghost(par):
         for n, X in enumerate((XA, XD)):
-            arrived(X.at[par, :, 0, 0:rows, :], r_x.at[par, n])
+            arrived(X[par].at[:, 0, 0:rows, :], r_x.at[par, n])
             for c in range(NL):
-                X[par, 2, 0, 8 * c : 8 * c + 8, :] = -X[par, 2, 0, 8 * c : 8 * c + 8, :]
+                X[par][2, 0, 8 * c : 8 * c + 8, :] = -X[par][2, 0, 8 * c : 8 * c + 8, :]
 
     coefs = chebyshev()
 
-    def sweep(s, _):
+    def element_forces(par, m, c):
+        u, v, w = modes(par, m, c)
+        e = EM[m, 8 * c : 8 * c + 8, :]
+        e2, e3, eq = e + e, e * (1.0 / 3.0), e * ((RATIO + 4.0) / 9.0)
+        tr = (0.5 * RATIO) * (u["x"] + v["y"] + w["z"])
+        fx = e2 * (tr + u["x"])
+        fy = e2 * (tr + v["y"])
+        fz = e2 * (tr + w["z"])
+        sxy = e * (u["y"] + v["x"])
+        syz = e * (v["z"] + w["y"])
+        szx = e * (u["z"] + w["x"])
+        h = 0.5 * (v["xy"] + w["zx"])
+        vxy, wzx = e * (v["xy"] + h), e * (w["zx"] + h)
+        h = 0.5 * (u["xy"] + w["yz"])
+        uxy, wyz = e * (u["xy"] + h), e * (w["yz"] + h)
+        h = 0.5 * (u["zx"] + v["yz"])
+        uzx, vyz = e * (u["zx"] + h), e * (v["yz"] + h)
+        h = u["yz"] + v["zx"] + w["xy"]
+        uyz, vzx, wxy = e3 * (u["yz"] + h), e3 * (v["zx"] + h), e3 * (w["xy"] + h)
+        uq, vq, wq = eq * u["xyz"], eq * v["xyz"], eq * w["xyz"]
+        return (
+            (szx, sxy, uyz, fx, uzx, uxy, uq),
+            (syz, fy, vyz, sxy, vzx, vxy, vq),
+            (fz, syz, wyz, szx, wzx, wxy, wq),
+        )
+
+    def push_up(comp, at, force):
+        gz_, gy, gyz, gx, gzx, gxy, gxyz = force
+        UP[4 * comp, at, :] = gz_
+        UP[4 * comp + 1, at, :] = gy + gyz
+        UP[4 * comp + 2, at, :] = gx + gzx
+        UP[4 * comp + 3, at, :] = gxy + gxyz
+
+    def sweep(s):
         par = s % 2
         nxt = 1 - par
-        c1, c2 = f32(coefs[0][0]), f32(coefs[0][1])
-        for n in range(1, SWEEPS):
-            c1 = jnp.where(s == n, f32(coefs[n][0]), c1)
-            c2 = jnp.where(s == n, f32(coefs[n][1]), c2)
-        last = jnp.where(s == SWEEPS - 1, f32(1.0), f32(0.0))
-        count = nodes - 1 - s
+        c1, c2 = coefs[s]
         ghost(par)
+        for c in range(NL):
+            at = slice(8 * c, 8 * c + 8)
+            for comp, force in enumerate(element_forces(par, 0, c)):
+                push_up(comp, at, force)
 
         def layer(m, _):
-            put = jnp.where(m == 0, 9, m)
             for c in range(NL):
                 at = slice(8 * c, 8 * c + 8)
-                u, v, w = modes(par, m, c)
-                e = EM[m, at, :]
-                e2, e3, eq = e + e, e * (1.0 / 3.0), e * ((RATIO + 4.0) / 9.0)
-                tr = (0.5 * RATIO) * (u["x"] + v["y"] + w["z"])
-                fx = e2 * (tr + u["x"])
-                fy = e2 * (tr + v["y"])
-                fz = e2 * (tr + w["z"])
-                sxy = e * (u["y"] + v["x"])
-                syz = e * (v["z"] + w["y"])
-                szx = e * (u["z"] + w["x"])
-                h = 0.5 * (v["xy"] + w["zx"])
-                vxy, wzx = e * (v["xy"] + h), e * (w["zx"] + h)
-                h = 0.5 * (u["xy"] + w["yz"])
-                uxy, wyz = e * (u["xy"] + h), e * (w["yz"] + h)
-                h = 0.5 * (u["zx"] + v["yz"])
-                uzx, vyz = e * (u["zx"] + h), e * (v["yz"] + h)
-                h = u["yz"] + v["zx"] + w["xy"]
-                uyz, vzx, wxy = e3 * (u["yz"] + h), e3 * (v["zx"] + h), e3 * (w["xy"] + h)
-                uq, vq, wq = eq * u["xyz"], eq * v["xyz"], eq * w["xyz"]
-                forces_of = (
-                    (szx, sxy, uyz, fx, uzx, uxy, uq),
-                    (syz, fy, vyz, sxy, vzx, vxy, vq),
-                    (fz, syz, wyz, szx, wzx, wxy, wq),
-                )
                 inv = INVD[m, at, :]
-                for comp in range(3):
-                    gz_, gy, gyz, gx, gzx, gxy, gxyz = forces_of[comp]
+                for comp, force in enumerate(element_forces(par, m, c)):
+                    gz_, gy, gyz, gx, gzx, gxy, gxyz = force
                     taa = UP[4 * comp, at, :] - gz_
                     tay = UP[4 * comp + 1, at, :] + (gy - gyz)
                     tda = UP[4 * comp + 2, at, :] + (gx - gzx)
                     tdy = UP[4 * comp + 3, at, :] + (gxy - gxyz)
-                    UP[4 * comp, at, :] = gz_
-                    UP[4 * comp + 1, at, :] = gy + gyz
-                    UP[4 * comp + 2, at, :] = gx + gzx
-                    UP[4 * comp + 3, at, :] = gxy + gxyz
+                    push_up(comp, at, force)
                     GU[2 * comp, 8 * c + 8 : 8 * c + 16, :] = taa + tay
                     GU[2 * comp + 1, 8 * c + 8 : 8 * c + 16, :] = tda + tdy
                     a = (taa - tay) + GU[2 * comp, 8 * c + 7 : 8 * c + 15, :]
                     b = (tda - tdy) + GU[2 * comp + 1, 8 * c + 7 : 8 * c + 15, :]
                     pushed = (a - b) + xprev(a + b)
                     res = R[comp, m, at, :] - pushed
-                    R[comp, put, at, :] = res
+                    R[comp, m, at, :] = res
                     step = c1 * STEP[comp, m, at, :] + c2 * (inv * res)
-                    STEP[comp, put, at, :] = step
-                    before = SOL[comp, m, at, :]
-                    SOL[comp, put, at, :] = before + step
-                    sent = step + last * before
+                    STEP[comp, m, at, :] = step
+                    sent = SOL[comp, m, at, :] + step
+                    SOL[comp, m, at, :] = sent
+                    if s < SWEEPS - 1:
+                        sent = step
                     n = xnext(sent)
-                    XA[nxt, comp, put, at, :] = sent + n
-                    XD[nxt, comp, put, at, :] = n - sent
+                    XA[nxt][comp, m, at, :] = sent + n
+                    XD[nxt][comp, m, at, :] = n - sent
 
             @pl.when(m == 1)
             def _():
@@ -464,20 +470,10 @@
 
             return 0
 
-        lax.fori_loop(0, count + 1, layer, 0)
-        return 0
-
-    for f in range(12):
-        for c in range(NL):
-            UP[f, 8 * c : 8 * c + 8, :] = zero8
-    for c in range(NL):
-        at = slice(8 * c, 8 * c + 8)
-        INVD[0, at, :] = zero8
-        for comp in range(3):
-            R[comp, 0, at, :] = zero8
-            STEP[comp, 0, at, :] = zero8
-            SOL[comp, 0, at, :] = zero8
-    lax.fori_loop(0, SWEEPS, sweep, 0)
+        lax.fori_loop(1, nodes - s, layer, 0)
+
+    for s in range(SWEEPS):
+        sweep(s)
 
     def lay_out(k, _):
         m = jnp.where(core == 1, k + 1, 4 - k)
@@ -692,8 +688,10 @@
             vm(3, 10, rows, 128),
             vm(3, 10, rows, 128),
             vm(3, 10, rows, 128),
-            vm(2, 3, 10, rows + 8, 128),
-            vm(2, 3, 10, rows + 8, 128),
+            vm(3, 10, rows + 8, 128),
+            vm(3, 10, rows + 8, 128),
+            vm(3, 10, rows + 8, 128),
+            vm(3, 10, rows + 8, 128),
             vm(12, rows, 128),
             vm(6, rows + 8, 128),
             vm(3, 4, rows, 128),

time: 83.5 us -> 58.2 us (0.70)
  the two profiles are of different devices: /device:TPU:6 before, /device:TPU:1 now
where the time goes in v1:
time: 58.2 us; the launch traced here: 57.9 us
  Pallas kernels  52.8 us (91%)
  local copies, waits for them, and re-layouts  4.53 us (8%)
  between operations  0.65 us (1%)
    pallas_call x1, Pallas kernels, on_device(): pl.pallas_call(functools.partial(kernel, NL, Z), out_shape=(jax.ShapeDtyp...  52.8 us
    unnamed x10, local copies, waits for them, and re-layouts  4.53 us

profile of v1, /device:TPU:1, one launch (start us, length us, event | category | flops | bytes accessed | tf_op | source)
XLA Modules:
  0.0 57.9 jit_solution(12178175729844126733)
XLA Ops:
  0.6 0.0 copy-start
  0.6 1.0 %copy-done = f32[2,3,2,64,128]{4,3,2,1,0:T(8,128)S(1)} copy-done((f32[2,3,2,64,128]{4,3,2,1,0:T(8,128)S(1)}, f32[2,3,2,64,128]{4,3,2,1,0:T(8,128)}, u32[]{:S(2)}) %copy-start) | copy-done | bytes 393240
  1.6 0.0 copy-start.1
  1.6 0.8 %copy-done.1 = s32[2,64,128]{2,1,0:T(8,128)S(1)} copy-done((s32[2,64,128]{2,1,0:T(8,128)S(1)}, s32[2,64,128]{2,1,0:T(8,128)}, u32[]{:S(2)}) %copy-start.1) | copy-done | bytes 65560
  2.5 0.0 copy-start.2
  2.5 0.7 %copy-done.2 = f32[2,8,128]{2,1,0:T(8,128)S(1)} copy-done((f32[2,8,128]{2,1,0:T(8,128)S(1)}, f32[2,8,128]{2,1,0:T(8,128)}, u32[]{:S(2)}) %copy-start.2) | copy-done | bytes 8216
  3.2 0.0 copy-start.3
  3.2 0.7 %copy-done.3 = s32[16]{0:T(128)S(1)} copy-done((s32[16]{0:T(128)S(1)}, s32[16]{0:T(128)}, u32[]{:S(2)}) %copy-start.3) | copy-done | bytes 88
  3.8 52.8 %step.1 = (f32[2,8,128]{2,1,0:T(8,128)S(1)}, f32[2,3,2,64,128]{4,3,2,1,0:T(8,128)S(1)}) custom-call(f32[2,8,128]{2,1,0:T(8,128)S(1)} %copy-done.2, s32[2,64,128]{2,1,0:T(8,128)S(1)} %copy-done.1, f32[2,3,2,64,128]{4,3,2,1,0:T(8,128)S(1)} %copy-done, s32[16]{0:T(128)S(1)} %copy-done.3), custom_call_target="tpu_custom_call" | custom-call | tf_op jit(solution)/shard_map/step/pallas_call | solution.py:720
  56.6 0.6 %copy.8 = f32[2,8,128]{2,1,0:T(8,128)} copy(f32[2,8,128]{2,1,0:T(8,128)S(1)} %get-tuple-element.4) | data formatting | bytes 16384
  57.2 0.7 %copy.9 = f32[2,3,2,64,128]{4,3,2,1,0:T(8,128)} copy(f32[2,3,2,64,128]{4,3,2,1,0:T(8,128)S(1)} %get-tuple-element.5) | data formatting | bytes 786432
Async XLA Ops:
  0.6 1.0 %copy-start = (f32[2,3,2,64,128]{4,3,2,1,0:T(8,128)S(1)}, f32[2,3,2,64,128]{4,3,2,1,0:T(8,128)}, u32[]{:S(2)}) copy-start(f32[2,3,2,64,128]{4,3,2,1,0:T(8,128)} %forces.1) | copy-start | bytes 1179652
  1.6 0.8 %copy-start.1 = (s32[2,64,128]{2,1,0:T(8,128)S(1)}, s32[2,64,128]{2,1,0:T(8,128)}, u32[]{:S(2)}) copy-start(s32[2,64,128]{2,1,0:T(8,128)} %labels.1) | copy-start | bytes 196612
  2.5 0.7 %copy-start.2 = (f32[2,8,128]{2,1,0:T(8,128)S(1)}, f32[2,8,128]{2,1,0:T(8,128)}, u32[]{:S(2)}) copy-start(f32[2,8,128]{2,1,0:T(8,128)} %density.1) | copy-start | bytes 24580
  3.2 0.7 %copy-start.3 = (s32[16]{0:T(128)S(1)}, s32[16]{0:T(128)}, u32[]{:S(2)}) copy-start(s32[16]{0:T(128)} %weights.1) | copy-start | bytes 196

commit v2 on v1

v2 whole, which is shorter than its diff:
```python
import functools

import jax
import jax.numpy as jnp
import numpy as np
from jax import lax
from jax.experimental import pallas as pl
from jax.experimental.pallas import tpu as pltpu
from jax.sharding import PartitionSpec as P

MESH = pl.DeviceIdType.MESH
SWEEPS = 3
EMIN = 0.001
LOWER_EIG = 0.1
UPPER_EIG = 2.5
MOVE_LIMIT = 0.2
FLOOR_DENSITY = 0.001
THETA = 0.5 * (UPPER_EIG + LOWER_EIG)
DELTA = 0.5 * (UPPER_EIG - LOWER_EIG)
POISSON = 0.3
SHEAR = 1.0 / (2 * (1 + POISSON))
RATIO = 2 * POISSON / (1 - 2 * POISSON)
UNIT = SHEAR / 16.0
DIAG = UNIT * ((RATIO + 4.0) + (2.0 * (RATIO + 3.0) + 2.0) / 3.0 + (RATIO + 4.0) / 9.0)
EDGE = 1.5 - float(np.sqrt(2.0))


def chebyshev():
    sigma = THETA / DELTA
    factor = 1.0 / sigma
    pairs = []
    for _ in range(SWEEPS):
        following = 1.0 / (2.0 * sigma - factor)
        pairs.append((following * factor, 2.0 * following / DELTA))
        factor = following
    return pairs


def kernel(
    NL, Z, density, labels, forces, weights_in, newd, disp,
    F, LAB, D, EM, TX, INVD, R, STEP, SOL, XA0, XA1, XD0, XD1, UP, GU, OUT, ZS, ZG,
    PA, PB, V, VO, G, MS, RX, DS, SV, RX2, weights, spare,
    s_d, r_d, s_e, r_e, s_f, r_f, s_l, r_l, s_v, r_v, s_x, r_x, s_z, r_z,
    s_o, r_o, s_m, r_m, s_h, r_h, s_s, r_s, loc,
):
    rows = 8 * NL
    f32 = jnp.float32
    XA, XD = (XA0, XA1), (XD0, XD1)
    l = lax.axis_index("load")
    g = lax.axis_index("gz")
    core = g % 2
    yh = (g // 2) % 2
    z = g // 4

    def dev(ll, zz, yy, cc):
        return (lax.rem(ll + NL, NL), (lax.rem(zz + Z, Z) * 2 + yy) * 2 + cc)

    def remote(src, dst, ssem, rsem, target):
        return pltpu.make_async_remote_copy(
            src_ref=src, dst_ref=dst, send_sem=ssem, recv_sem=rsem, device_id=target, device_id_type=MESH
        )

    def arrived(ref, sem):
        pltpu.make_async_copy(ref, ref, sem).wait()

    pending = []
    lane = lax.broadcasted_iota(jnp.int32, (8, 128), 1)

    def xnext(v):
        return jnp.where(lane == 127, 0.0, pltpu.roll(v, 127, 1))

    def xprev(v):
        return jnp.where(lane == 0, 0.0, pltpu.roll(v, 1, 1))

    barrier = pltpu.get_barrier_semaphore()

    def greet(target):
        pl.semaphore_signal(barrier, inc=1, device_id=target, device_id_type=MESH)

    both = yh == core
    flipped = l + 1 - 2 * (l % 2)
    far = z + 2 * core - 1
    for a, b in ((0, 1), (1, 0), (1, 1)):
        greet(dev(l, z, (yh + a) % 2, (core + b) % 2))
    combos = [(t, a, b) for t in range(2) for a in range(2) for b in range(2)][1:]
    for t, a, b in combos:
        yy = (yh + a) % 2
        greet(dev(flipped if t else l, z + b * (core - yy), yy, (core + b) % 2))
    greet(dev(l, far, 1 - core, 1 - core))
    greet(dev(l, far, yh, 1 - core))
    for k in range(1, NL // 2):
        greet(dev(l + 2 * k, z, yh, core))
    for k in range(1, Z):
        greet(dev(l, z + k, yh, core))
    pl.semaphore_wait(barrier, 11 + (NL // 2 - 1) + (Z - 1) + jnp.where(both, 2, 0))

    mine = pl.ds(pl.multiple_of(8 * l, 8), 8)
    here8 = pl.ds(pl.multiple_of(8 * l + 8, 8), 8)
    quarter = 2 * yh + core
    block_of = [(quarter + 1) % 4, (quarter + 3) % 4]
    block = [jnp.where(core == 0, block_of[0], block_of[1]), jnp.where(core == 0, block_of[1], block_of[0])]

    def holder(t, a, b):
        return dev(flipped if t else l, z + b * (core + yh - 1), (yh + a) % 2, (core + b) % 2)

    for n, (t, a, b) in enumerate(combos):
        cp = remote(density, D.at[pl.ds(2 * block[b], 2), here8, :], s_d.at[n], r_d, holder(t, a, b))
        cp.start()
        pending.append(cp.wait_send)
    pltpu.make_async_copy(density, D.at[pl.ds(2 * block[0], 2), here8, :], r_d).start()

    def l_make(n, two):
        a, b = ((1, 0), (0, 1), (1, 1))[n]
        if two:
            src, dst = labels, LAB.at[pl.ds(2 * block[b], 2)]
        else:
            src, dst = labels.at[core], LAB.at[2 * block[b] + core]
        return remote(src, dst, s_l.at[n], r_l.at[block[b]], holder(a, a, b))

    def l_each(act):
        @pl.when(both)
        def _():
            act(l_make(0, True))

        @pl.when(quarter == 1)
        def _():
            act(l_make(0, False))

        for n in (1, 2):
            @pl.when(quarter == 0)
            def _():
                act(l_make(n, False))

            @pl.when(quarter != 0)
            def _():
                act(l_make(n, True))

    l_each(lambda cp: cp.start())
    pending.append(lambda: l_each(lambda cp: cp.wait_send()))
    pltpu.make_async_copy(labels, LAB.at[pl.ds(2 * block[0], 2)], r_l.at[block[0]]).start()

    is_self = [jnp.logical_and(both, yh == 0), jnp.logical_and(both, yh == 1)]

    def f_make(k):
        return remote(
            forces.at[k], F.at[:, pl.ds(2 * core, 2)], s_f.at[0, k], r_f.at[core], dev(l, z, k, yh)
        )

    def f_far(k):
        return remote(
            forces.at[k, :, yh], F.at[:, 4], s_f.at[1, k], r_f.at[2], dev(l, z + 2 * yh - 1, k, 1 - yh)
        )

    def f_sent():
        for k in range(2):
            @pl.when(jnp.logical_not(is_self[k]))
            def _():
                f_make(k).wait_send()

        @pl.when(both)
        def _():
            for k in range(2):
                f_far(k).wait_send()

    pending.append(f_sent)
    get_weights = pltpu.make_async_copy(weights_in, weights, loc.at[0])
    get_weights.start()

    zero8 = jnp.zeros((8, 128), f32)
    for r in range(8):
        D[r, 0:8, :] = zero8
        D[r, rows + 8 : rows + 16, :] = zero8
    for r in range(6):
        V[r, 0:8, :] = zero8
        V[r, rows + 8 : rows + 16, :] = zero8
        TX[r, 0:8, :] = zero8
        GU[r, 0:8, :] = zero8
        for k in range(2):
            for c in range(3):
                XA[k][c, r, rows : rows + 8, :] = zero8
                XD[k][c, r, rows : rows + 8, :] = zero8
    for k in range(4):
        for t in range(3):
            DS[k, 8 * t : 8 * t + 8, :] = zero8
    for c in range(NL):
        for k in range(2):
            MS[c, k, 2] = zero8

    own16 = l // 2

    def strip(x):
        return D.at[:, pl.ds(pl.multiple_of(16 * x + 8, 8), 16), :]

    arrived(strip(own16), r_d)
    for k in range(1, NL // 2):
        cp = remote(strip(own16), strip(own16), s_e.at[k - 1], r_e.at[k - 1], dev(l + 2 * k, z, yh, core))
        cp.start()
        pending.append(cp.wait_send)
    for k in range(2):
        @pl.when(is_self[k])
        def _():
            pltpu.make_async_copy(forces.at[k], F.at[:, pl.ds(2 * core, 2)], r_f.at[core]).start()

        @pl.when(jnp.logical_not(is_self[k]))
        def _():
            f_make(k).start()

    @pl.when(both)
    def _():
        for k in range(2):
            f_far(k).start()

    for k in range(1, NL // 2):
        arrived(strip(lax.rem(own16 + NL // 2 - k, NL // 2)), r_e.at[k - 1])

    @pl.when(jnp.logical_or(core == 0, yh == 0))
    def _():
        arrived(LAB.at[0:2], r_l.at[0])

    @pl.when(quarter == 3)
    def _():
        arrived(LAB.at[1], r_l.at[0])

    for b in (1, 2):
        arrived(LAB.at[2 * b : 2 * b + 2], r_l.at[b])

    @pl.when(core == 1)
    def _():
        arrived(LAB.at[6], r_l.at[3])

    @pl.when(quarter == 2)
    def _():
        arrived(LAB.at[6:8], r_l.at[3])

    sibling = dev(l, z, yh, 1 - core)

    sgn = 2 * core - 1

    def inside(p):
        at = 8 * z + p
        return jnp.logical_and(at >= 0, at < 8 * Z)

    def moduli_layer(m, _):
        p = 3 + sgn * m
        r = p + 2 - 4 * core
        scale = jnp.where(inside(p), f32(UNIT), f32(0.0))
        for c in range(NL):
            d = D[r, 8 * c + 8 : 8 * c + 16, :]
            solid = jnp.where(LAB[r, 8 * c : 8 * c + 8, :] == 2, 1.0, d)
            e = (EMIN + (1.0 - EMIN) * solid * solid * solid) * scale
            EM[m, 8 * c : 8 * c + 8, :] = e
            TX[m, 8 * c + 8 : 8 * c + 16, :] = e + xprev(e)
        return 0

    lax.fori_loop(0, 6, moduli_layer, 0)

    def inverse_layer(m, _):
        p = jnp.where(core == 1, 3 + m, 4 - m)
        r = p + 2 - 4 * core
        keep = jnp.where(inside(p), 1, 0)
        for c in range(NL):
            near = TX[m, 8 * c + 8 : 8 * c + 16, :] + TX[m, 8 * c + 7 : 8 * c + 15, :]
            back = TX[m - 1, 8 * c + 8 : 8 * c + 16, :] + TX[m - 1, 8 * c + 7 : 8 * c + 15, :]
            lab = LAB[r, 8 * c : 8 * c + 8, :] * keep + (1 - keep)
            INVD[m, 8 * c : 8 * c + 8, :] = jnp.where(lab != 1, (UNIT / DIAG) / (near + back), 0.0)
        return 0

    lax.fori_loop(1, 6, inverse_layer, 0)

    def plane_sums(center, above, below):
        ysum = above + below
        xsum = xnext(center) + xprev(center)
        cross = ysum + xsum
        corner = xnext(ysum) + xprev(ysum)
        return 1.5 * center + 0.5 * cross + EDGE * corner, 0.5 * center + EDGE * cross

    def d_plane(r, _):
        scale = jnp.where(inside(r - 2 + 4 * core), f32(1.0), f32(0.0))
        for c in range(NL):
            a, b = plane_sums(
                D[r, 8 * c + 8 : 8 * c + 16, :], D[r, 8 * c + 7 : 8 * c + 15, :], D[r, 8 * c + 9 : 8 * c + 17, :]
            )
            PA[r, 8 * c : 8 * c + 8, :] = a * scale
            PB[r, 8 * c : 8 * c + 8, :] = b * scale
        return 0

    def v_plane(r, _):
        ok = jnp.where(inside(r - 2 + 4 * core), f32(1.0), f32(0.0))
        for c in range(NL):
            at = slice(8 * c, 8 * c + 8)
            total = PA[r, at, :] + PB[r - 1, at, :] + PB[r + 1, at, :]
            V[r - 1, 8 * c + 8 : 8 * c + 16, :] = ok / (total + (1.0 - ok))
        return 0

    def v_make():
        return remote(V.at[pl.ds(3 - 2 * core, 2), here8, :], VO, s_v, r_v, sibling)

    def v_sent():
        @pl.when(both)
        def _():
            v_make().wait_send()

    def w_plane(n, _):
        for c in range(NL):
            a, b = plane_sums(
                V[n, 8 * c + 8 : 8 * c + 16, :], V[n, 8 * c + 7 : 8 * c + 15, :], V[n, 8 * c + 9 : 8 * c + 17, :]
            )
            PA[n, 8 * c : 8 * c + 8, :] = a
            PB[n, 8 * c : 8 * c + 8, :] = b
        return 0

    def g_plane(k, _):
        r = k + 2
        for c in range(NL):
            at = slice(8 * c, 8 * c + 8)
            d = D[r, 8 * c + 8 : 8 * c + 16, :]
            solid = jnp.where(LAB[r, at, :] == 2, 1.0, d)
            G[k, at, :] = (PA[k + 1, at, :] + PB[k, at, :] + PB[k + 2, at, :]) * (d * solid * solid)
        return 0

    def filter_part(s):
        if s == 1:
            lax.fori_loop(0, 8, d_plane, 0)
            lax.fori_loop(1, 7, v_plane, 0)

            @pl.when(both)
            def _():
                v_make().start()
        elif s == 2:
            lax.fori_loop(0, 6, w_plane, 0)
            lax.fori_loop(0, 4, g_plane, 0)

    for k in range(2):
        arrived(F.at[:, 2 * k : 2 * k + 2], r_f.at[k])
    arrived(F.at[:, 4], r_f.at[2])
    flip = jnp.where(core == 1, f32(1.0), f32(-1.0))

    def x_make(par):
        return [
            remote(X[par].at[:, 1, 0:rows, :], X[par].at[:, 0, 0:rows, :], s_x.at[par, n], r_x.at[par, n], sibling)
            for n, X in enumerate((XA, XD))
        ]

    def first_step(m, _):
        i = jnp.where(jnp.logical_or(core == 1, m == 5), m - 1, 4 - m)
        for c in range(NL):
            at = slice(8 * c, 8 * c + 8)
            inv = INVD[m, at, :]
            for comp in range(3):
                f = F[comp, i, at, :]
                if comp == 2:
                    f = f * flip
                R[comp, m, at, :] = f
                s = inv * f * (1.0 / THETA)
                STEP[comp, m, at, :] = s
                SOL[comp, m, at, :] = s
                n = xnext(s)
                XA[0][comp, m, at, :] = s + n
                XD[0][comp, m, at, :] = n - s

        @pl.when(m == 1)
        def _():
            for cp in x_make(0):
                cp.start()

        return 0

    lax.fori_loop(1, 6, first_step, 0)

    def fields(par, comp, m, c):
        a0 = XA[par][comp, m, 8 * c : 8 * c + 8, :]
        a1 = XA[par][comp, m, 8 * c + 1 : 8 * c + 9, :]
        d0 = XD[par][comp, m, 8 * c : 8 * c + 8, :]
        d1 = XD[par][comp, m, 8 * c + 1 : 8 * c + 9, :]
        return a0 + a1, a1 - a0, d0 + d1, d1 - d0

    def modes(par, m, c):
        out = []
        for comp in range(3):
            lo = fields(par, comp, m, c)
            hi = fields(par, comp, m + 1, c)
            out.append(
                dict(
                    z=hi[0] - lo[0], y=hi[1] + lo[1], yz=hi[1] - lo[1], x=hi[2] + lo[2], zx=hi[2] - lo[2],
                    xy=hi[3] + lo[3], xyz=hi[3] - lo[3],
                )
            )
        return out

    def ghost(par):
        for n, X in enumerate((XA, XD)):
            arrived(X[par].at[:, 0, 0:rows, :], r_x.at[par, n])
            for c in range(NL):
                X[par][2, 0, 8 * c : 8 * c + 8, :] = -X[par][2, 0, 8 * c : 8 * c + 8, :]

    there = jnp.where(inside(jnp.where(core == 1, 8, -1)), f32(1.0), f32(0.0))

    def z_make(par):
        return remote(ZS.at[par], ZG.at[par], s_z.at[par], r_z.at[par], dev(l, far, yh, 1 - core))

    def far_ghost(par):
        arrived(ZG.at[par], r_z.at[par])
        for comp in range(3):
            scale = -there if comp == 2 else there
            for c in range(NL):
                at = slice(8 * c, 8 * c + 8)
                v = ZG[par, comp, at, :] * scale
                n = xnext(v)
                XA[par][comp, 5, at, :] = v + n
                XD[par][comp, 5, at, :] = n - v

    def lay_out(half):
        for n in range(2):
            k = 2 * half + n
            m = jnp.where(core == 1, k + 1, 4 - k)
            for c in range(NL):
                at = slice(8 * c, 8 * c + 8)
                for comp in range(3):
                    v = SOL[comp, m, at, :]
                    OUT[comp, k, at, :] = v * flip if comp == 2 else v

    def o_make(half):
        return remote(
            OUT.at[:, pl.ds(2 * half, 2)], disp.at[yh], s_o.at[half], r_o.at[yh], dev(l, z, core, half)
        )

    coefs = chebyshev()

    def element_forces(par, m, c):
        u, v, w = modes(par, m, c)
        e = EM[m, 8 * c : 8 * c + 8, :]
        e2, e3, eq = e + e, e * (1.0 / 3.0), e * ((RATIO + 4.0) / 9.0)
        tr = (0.5 * RATIO) * (u["x"] + v["y"] + w["z"])
        fx = e2 * (tr + u["x"])
        fy = e2 * (tr + v["y"])
        fz = e2 * (tr + w["z"])
        sxy = e * (u["y"] + v["x"])
        syz = e * (v["z"] + w["y"])
        szx = e * (u["z"] + w["x"])
        h = 0.5 * (v["xy"] + w["zx"])
        vxy, wzx = e * (v["xy"] + h), e * (w["zx"] + h)
        h = 0.5 * (u["xy"] + w["yz"])
        uxy, wyz = e * (u["xy"] + h), e * (w["yz"] + h)
        h = 0.5 * (u["zx"] + v["yz"])
        uzx, vyz = e * (u["zx"] + h), e * (v["yz"] + h)
        h = u["yz"] + v["zx"] + w["xy"]
        uyz, vzx, wxy = e3 * (u["yz"] + h), e3 * (v["zx"] + h), e3 * (w["xy"] + h)
        uq, vq, wq = eq * u["xyz"], eq * v["xyz"], eq * w["xyz"]
        return (
            (szx, sxy, uyz, fx, uzx, uxy, uq),
            (syz, fy, vyz, sxy, vzx, vxy, vq),
            (fz, syz, wyz, szx, wzx, wxy, wq),
        )

    def push_up(comp, at, force):
        gz_, gy, gyz, gx, gzx, gxy, gxyz = force
        UP[4 * comp, at, :] = gz_
        UP[4 * comp + 1, at, :] = gy + gyz
        UP[4 * comp + 2, at, :] = gx + gzx
        UP[4 * comp + 3, at, :] = gxy + gxyz

    def sweep(s):
        par = s % 2
        nxt = 1 - par
        c1, c2 = coefs[s]
        ghost(par)
        for c in range(NL):
            at = slice(8 * c, 8 * c + 8)
            for comp, force in enumerate(element_forces(par, 0, c)):
                push_up(comp, at, force)

        def layer(m, _):
            if s > 0:
                @pl.when(m == 4)
                def _():
                    if s == SWEEPS - 1:
                        lay_out(1 - core)
                        o_make(1 - core).start()
                    filter_part(s)
                    far_ghost(par)

            for c in range(NL):
                at = slice(8 * c, 8 * c + 8)
                inv = INVD[m, at, :]
                for comp, force in enumerate(element_forces(par, m, c)):
                    gz_, gy, gyz, gx, gzx, gxy, gxyz = force
                    taa = UP[4 * comp, at, :] - gz_
                    tay = UP[4 * comp + 1, at, :] + (gy - gyz)
                    tda = UP[4 * comp + 2, at, :] + (gx - gzx)
                    tdy = UP[4 * comp + 3, at, :] + (gxy - gxyz)
                    push_up(comp, at, force)
                    GU[2 * comp, 8 * c + 8 : 8 * c + 16, :] = taa + tay
                    GU[2 * comp + 1, 8 * c + 8 : 8 * c + 16, :] = tda + tdy
                    a = (taa - tay) + GU[2 * comp, 8 * c + 7 : 8 * c + 15, :]
                    b = (tda - tdy) + GU[2 * comp + 1, 8 * c + 7 : 8 * c + 15, :]
                    pushed = (a - b) + xprev(a + b)
                    res = R[comp, m, at, :] - pushed
                    R[comp, m, at, :] = res
                    step = c1 * STEP[comp, m, at, :] + c2 * (inv * res)
                    STEP[comp, m, at, :] = step
                    sent = SOL[comp, m, at, :] + step
                    SOL[comp, m, at, :] = sent
                    if s < SWEEPS - 1:
                        sent = step
                    n = xnext(sent)
                    XA[nxt][comp, m, at, :] = sent + n
                    XD[nxt][comp, m, at, :] = n - sent

            @pl.when(m == 1)
            def _():
                for cp in x_make(par):
                    cp.wait_send()
                for cp in x_make(nxt):
                    cp.start()

            @pl.when(m == 4)
            def _():
                if s > 0:
                    z_make(par).wait_send()
                for comp in range(3):
                    for c in range(NL):
                        at = slice(8 * c, 8 * c + 8)
                        ZS[nxt, comp, at, :] = (STEP if s < SWEEPS - 1 else SOL)[comp, 4, at, :]
                if s < SWEEPS - 1:
                    z_make(nxt).start()
                else:
                    @pl.when(core == 0)
                    def _():
                        z_make(nxt).start()

            return 0

        lax.fori_loop(1, 5, layer, 0)

    for s in range(SWEEPS):
        sweep(s)

    @pl.when(both)
    def _():
        lay_out(core)
        pltpu.make_async_copy(OUT.at[:, pl.ds(2 * core, 2)], disp.at[yh], r_o.at[yh]).start()

    @pl.when(jnp.logical_not(both))
    def _():
        lay_out(core)
        o_make(core).start()

    def o_ended():
        o_make(1 - core).wait_send()

        @pl.when(jnp.logical_not(both))
        def _():
            o_make(core).wait_send()

        for k in range(2):
            arrived(disp.at[k], r_o.at[k])

    pending.append(o_ended)

    fin = SWEEPS % 2
    get_weights.wait()
    pending.extend(cp.wait_send for cp in x_make(fin))
    pending.append(v_sent)

    def z_sent():
        @pl.when(core == 0)
        def _():
            z_make(fin).wait_send()

    pending.append(z_sent)
    weight = weights[2 * l + yh].astype(f32)
    weight_sum = weights[0]
    for n in range(1, 2 * NL):
        weight_sum = weight_sum + weights[n]
    weight_sum = weight_sum.astype(f32)

    def energy_layer(k, share):
        m = jnp.where(core == 1, k + 1, 3 - k)
        for c in range(NL):
            u, v, w = modes(fin, m, c)
            tr = u["x"] + v["y"] + w["z"]
            sq = lambda t: t * t
            normal = sq(u["x"]) + sq(v["y"]) + sq(w["z"])
            shear = sq(u["y"] + v["x"]) + sq(v["z"] + w["y"]) + sq(u["z"] + w["x"])
            pairs = (
                sq(v["xy"]) + sq(w["zx"]) + sq(u["xy"]) + sq(w["yz"]) + sq(u["zx"]) + sq(v["yz"])
            )
            joint = sq(v["xy"] + w["zx"]) + sq(u["xy"] + w["yz"]) + sq(u["zx"] + v["yz"])
            s = u["yz"] + v["zx"] + w["xy"]
            triple = sq(u["yz"]) + sq(v["zx"]) + sq(w["xy"]) + sq(s)
            quad = sq(u["xyz"]) + sq(v["xyz"]) + sq(w["xyz"])
            total = (
                (RATIO * sq(tr) + 2.0 * normal + shear) + (pairs + 0.5 * joint)
                + (1.0 / 3.0) * triple + ((RATIO + 4.0) / 9.0) * quad
            )
            t = (weight * UNIT) * total
            half, j = k // 2, k % 2
            MS[c, half, j] = t
            if c > 0:
                MS[c - 1, half, 2, pl.ds(2 * j + 1, 1), :] = t[0:1, :]
            if c < NL - 1:
                MS[c + 1, half, 2, pl.ds(2 * j, 1), :] = t[7:8, :]
            share = share + t * G[k, 8 * c : 8 * c + 8, :]
        return share

    def last_layer(k, got):
        @pl.when(k == 3)
        def _():
            ghost(fin)

            @pl.when(core == 1)
            def _():
                far_ghost(fin)

        return energy_layer(k, got)

    share = lax.fori_loop(0, 4, last_layer, zero8)
    share = jnp.sum(share, axis=0, keepdims=True)
    for c in range(NL):
        for k in range(2):
            MS[c, k, 2, 4:5, :] = share

    me = 2 * l + yh
    m_copies = []
    def m_make(k, cc):
        ll = lax.rem(l + k, NL)
        return remote(MS.at[ll, cc], RX.at[me], s_m.at[k, cc], r_m, dev(ll, z, core, cc))

    for k in range(NL):
        for cc in range(2):
            if k > 0:
                m_make(k, cc).start()
            else:
                alone = jnp.logical_and(both, core == cc)

                @pl.when(alone)
                def _():
                    pltpu.make_async_copy(MS.at[l, cc], RX.at[me], r_m).start()

                @pl.when(jnp.logical_not(alone))
                def _():
                    m_make(k, cc).start()

    def m_sent():
        for k in range(NL):
            for cc in range(2):
                if k > 0:
                    m_make(k, cc).wait_send()
                else:
                    @pl.when(jnp.logical_not(jnp.logical_and(both, core == cc)))
                    def _():
                        m_make(k, cc).wait_send()

    pending.append(m_sent)

    arrived(RX, r_m)
    scale = (3.0 * (1.0 - EMIN)) / weight_sum
    sums = []
    for k in range(3):
        part = RX[0, k]
        for n in range(1, 2 * NL):
            part = part + RX[n, k]
        sums.append(part)
    rim = sums[2]
    SV[...] = rim[4:5, :]

    def s_make(kz, ky):
        return remote(SV, RX2.at[2 * z + yh], s_s.at[kz, ky], r_s, dev(l, z + kz, (yh + ky) % 2, core))

    for kz in range(Z):
        for ky in range(2):
            if (kz, ky) != (0, 0):
                s_make(kz, ky).start()
    pltpu.make_async_copy(SV, RX2.at[2 * z + yh], r_s).start()

    def s_sent():
        for kz in range(Z):
            for ky in range(2):
                if (kz, ky) != (0, 0):
                    s_make(kz, ky).wait_send()

    pending.append(s_sent)
    native = 4 * yh + 2 * (1 - core)
    for k in range(2):
        main = sums[k]
        rated = []
        for n in range(3):
            near = pl.ds(pl.multiple_of(8 * l + 8 * n, 8), 8)
            d = D[native + k, near, :]
            row = jnp.clip(8 * l + 8 * (n - 1), 0, rows - 8)
            lab = LAB[native + k, pl.ds(pl.multiple_of(row, 8), 8), :]
            solid = jnp.where(lab == 2, 1.0, d)
            rated.append(d * solid * solid * scale)
        above = jnp.where(l > 0, f32(1.0), f32(0.0)) * rated[0][7:8, :]
        below = jnp.where(l < NL - 1, f32(1.0), f32(0.0)) * rated[2][0:1, :]
        DS[k + 1, 8:16, :] = main * rated[1]
        DS[k + 1, 7:8, :] = rim[2 * k : 2 * k + 1, :] * above
        DS[k + 1, 16:17, :] = rim[2 * k + 1 : 2 * k + 2, :] * below

    def h_make(up):
        to = lax.rem(g + (1 if up else 4 * Z - 1), 4 * Z)
        return remote(DS.at[2 if up else 1], DS.at[0 if up else 3], s_h.at[int(up)], r_h.at[int(up)], (l, to))

    for up in (False, True):
        h_make(up).start()
        pending.append(h_make(up).wait_send)
    arrived(DS.at[3], r_h.at[0])
    arrived(DS.at[0], r_h.at[1])

    planes = []
    for k in range(4):
        planes.append(plane_sums(DS[k, 8:16, :], DS[k, 7:15, :], DS[k, 9:17, :]))
    low = jnp.where(g > 0, f32(1.0), f32(0.0)) * planes[0][1]
    high = jnp.where(g < 4 * Z - 1, f32(1.0), f32(0.0)) * planes[3][1]
    numer = [planes[1][0] + low + planes[2][1], planes[2][0] + planes[1][1] + high]
    @pl.when(both)
    def _():
        for k in range(2):
            VO[k] = V[1 + 2 * core + k, here8, :]

    @pl.when(jnp.logical_not(both))
    def _():
        arrived(VO, r_v)

    arrived(RX2, r_s)
    total = RX2[0]
    for n in range(1, 2 * Z):
        total = total + RX2[n]
    mean = jnp.sum(total, axis=1, keepdims=True) * scale / (8 * Z * rows * 128)
    for k in range(2):
        filtered = numer[k] * VO[k]
        d = D[native + k, here8, :]
        candidate = d * jnp.sqrt(filtered / mean)
        lower = jnp.maximum(d - MOVE_LIMIT, FLOOR_DENSITY)
        upper = jnp.minimum(d + MOVE_LIMIT, 1.0)
        new = jnp.minimum(jnp.maximum(candidate, lower), upper)
        newd[k] = jnp.where(LAB[native + k, mine, :] == 2, 1.0, new)

    for end in pending:
        end()


def solution(mesh):
    NL, Z = mesh.shape["load"], mesh.shape["gz"] // 4
    rows = 8 * NL

    def on_device(density, labels, forces, case_weights):
        vm = lambda *shape: pltpu.VMEM(shape, jnp.float32)
        dma = lambda *shape: pltpu.SemaphoreType.DMA(shape)
        scratch = [
            vm(3, 5, rows, 128),
            pltpu.VMEM((8, rows, 128), jnp.int32),
            vm(8, rows + 16, 128),
            vm(6, rows, 128),
            vm(6, rows + 8, 128),
            vm(6, rows, 128),
            vm(3, 6, rows, 128),
            vm(3, 6, rows, 128),
            vm(3, 6, rows, 128),
            vm(3, 6, rows + 8, 128),
            vm(3, 6, rows + 8, 128),
            vm(3, 6, rows + 8, 128),
            vm(3, 6, rows + 8, 128),
            vm(12, rows, 128),
            vm(6, rows + 8, 128),
            vm(3, 4, rows, 128),
            vm(2, 3, rows, 128),
            vm(2, 3, rows, 128),
            vm(8, rows, 128),
            vm(8, rows, 128),
            vm(6, rows + 16, 128),
            vm(2, 8, 128),
            vm(4, rows, 128),
            vm(NL, 2, 3, 8, 128),
            vm(2 * NL, 3, 8, 128),
            vm(4, 24, 128),
            vm(1, 128),
            vm(2 * Z, 1, 128),
            pltpu.SMEM((2 * NL,), jnp.int32),
            vm(46 << 11, 128),
            dma(7), pltpu.SemaphoreType.DMA,
            dma(NL // 2), dma(NL // 2),
            dma(2, 2), dma(3),
            dma(3), dma(4),
            pltpu.SemaphoreType.DMA, pltpu.SemaphoreType.DMA,
            dma(2, 2), dma(2, 2),
            dma(2), dma(2),
            dma(2), dma(2),
            dma(NL, 2), pltpu.SemaphoreType.DMA,
            dma(2), dma(2),
            dma(Z, 2), pltpu.SemaphoreType.DMA,
            dma(1),
        ]
        return pl.pallas_call(
            functools.partial(kernel, NL, Z),
            out_shape=(
                pltpu.VMEM(density.shape, jnp.float32),
                pltpu.VMEM(forces.shape, jnp.float32),
            ),
            in_specs=[pl.BlockSpec(memory_space=pltpu.HBM)] * 4,
            out_specs=(pl.BlockSpec(memory_space=pltpu.VMEM), pl.BlockSpec(memory_space=pltpu.VMEM)),
            scratch_shapes=scratch,
            compiler_params=pltpu.CompilerParams(
                collective_id=1, has_side_effects=True, vmem_limit_bytes=60 << 20
            ),
            name="step",
        )(density, labels, forces, case_weights)

    return jax.shard_map(
        on_device,
        mesh=mesh,
        in_specs=(
            P("gz", "load", None),
            P("gz", None, None),
            P("load", None, "gz", None, None),
            P(),
        ),
        out_specs=(P("gz", "load", None), P("load", None, "gz", None, None)),
        check_vma=False,
    )
```

time: 58.2 us -> 49.5 us (0.85)
  Pallas kernels: 52.8 us -> 47.5 us
  local copies, waits for them, and re-layouts: 4.53 us -> 1.35 us
    pallas_call x1, Pallas kernels: 52.8 us -> 47.5 us  [on_device(): pl.pallas_call(functools.partial(kernel, NL, Z), out_shape=(pltpu.VMEM(de...]
    unnamed x10 -> x2, local copies, waits for them, and re-layouts: 4.53 us -> 1.35 us
where the time goes in v2:
time: 49.5 us
  Pallas kernels  47.5 us (96%)
  local copies, waits for them, and re-layouts  1.35 us (3%)
  between operations  0.64 us (1%)
    pallas_call x1, Pallas kernels, on_device(): pl.pallas_call(functools.partial(kernel, NL, Z), out_shape=(pltpu.VMEM(de...  47.5 us
    unnamed x2, local copies, waits for them, and re-layouts  1.35 us

profile of v2, /device:TPU:1, one launch (start us, length us, event | category | flops | bytes accessed | tf_op | source)
XLA Modules:
  0.0 49.5 jit_solution(7594657575151849950)
XLA Ops:
  0.6 47.5 %step.1 = (f32[2,8,128]{2,1,0:T(8,128)S(1)}, f32[2,3,2,64,128]{4,3,2,1,0:T(8,128)S(1)}) custom-call(f32[2,8,128]{2,1,0:T(8,128)} %density.1, s32[2,64,128]{2,1,0:T(8,128)} %labels.1, f32[2,3,2,64,128]{4,3,2,1,0:T(8,128)} %forces.1, s32[16]{0:T(128)} %weights_in.1), custom_call_target="tpu_custom_call" | custom-call | tf_op jit(solution)/shard_map/step/pallas_call | solution.py:794
  48.1 0.6 %copy.8 = f32[2,8,128]{2,1,0:T(8,128)} copy(f32[2,8,128]{2,1,0:T(8,128)S(1)} %get-tuple-element.2) | data formatting | bytes 16384
  48.7 0.7 %copy.9 = f32[2,3,2,64,128]{4,3,2,1,0:T(8,128)} copy(f32[2,3,2,64,128]{4,3,2,1,0:T(8,128)S(1)} %get-tuple-element.3) | data formatting | bytes 786432

commit v3 on v2

--- a/solution.py
+++ b/solution.py
@@ -37,10 +37,10 @@
 
 
 def kernel(
-    NL, Z, density, labels, forces, weights_in, newd, disp,
-    F, LAB, D, EM, TX, INVD, R, STEP, SOL, XA0, XA1, XD0, XD1, UP, GU, OUT, ZS, ZG,
+    NL, Z, density_in, labels_in, forces_in, weights_in, newd, disp,
+    density, labels, forces, F, LAB, D, EM, TX, INVD, R, STEP, SOL, XA0, XA1, XD0, XD1, UP, GU, GV, KU, OUT, ZS, ZG,
     PA, PB, V, VO, G, MS, RX, DS, SV, RX2, weights, spare,
-    s_d, r_d, s_e, r_e, s_f, r_f, s_l, r_l, s_v, r_v, s_x, r_x, s_z, r_z,
+    s_d, r_d, s_e, r_e, s_f, r_f, s_l, r_l, s_y, r_y, s_w, r_w, s_i, r_i, s_v, r_v, s_x, r_x, s_z, r_z,
     s_o, r_o, s_m, r_m, s_h, r_h, s_s, r_s, loc,
 ):
     rows = 8 * NL
@@ -64,6 +64,10 @@
         pltpu.make_async_copy(ref, ref, sem).wait()
 
     pending = []
+
+    def far_first(count):
+        return sorted(range(count), key=lambda k: -min(k, count - k))
+
     lane = lax.broadcasted_iota(jnp.int32, (8, 128), 1)
 
     def xnext(v):
@@ -72,100 +76,81 @@
     def xprev(v):
         return jnp.where(lane == 0, 0.0, pltpu.roll(v, 1, 1))
 
+    staged = [
+        pltpu.make_async_copy(given, here, loc.at[n])
+        for n, (given, here) in enumerate(
+            ((density_in, density), (labels_in, labels), (forces_in, forces), (weights_in, weights))
+        )
+    ]
+    for cp in staged:
+        cp.start()
     barrier = pltpu.get_barrier_semaphore()
 
     def greet(target):
         pl.semaphore_signal(barrier, inc=1, device_id=target, device_id_type=MESH)
 
     both = yh == core
-    flipped = l + 1 - 2 * (l % 2)
     far = z + 2 * core - 1
-    for a, b in ((0, 1), (1, 0), (1, 1)):
-        greet(dev(l, z, (yh + a) % 2, (core + b) % 2))
-    combos = [(t, a, b) for t in range(2) for a in range(2) for b in range(2)][1:]
-    for t, a, b in combos:
-        yy = (yh + a) % 2
-        greet(dev(flipped if t else l, z + b * (core - yy), yy, (core + b) % 2))
-    greet(dev(l, far, 1 - core, 1 - core))
+    sibling = dev(l, z, yh, 1 - core)
+    is_self = [jnp.logical_and(both, yh == 0), jnp.logical_and(both, yh == 1)]
+
+    for k in range(NL):
+        for cc in range(2):
+            if k > 0:
+                greet(dev(l + k, z, core, cc))
+            else:
+                @pl.when(jnp.logical_not(jnp.logical_and(both, core == cc)))
+                def _():
+                    greet(dev(l, z, core, cc))
+    greet(sibling)
     greet(dev(l, far, yh, 1 - core))
-    for k in range(1, NL // 2):
-        greet(dev(l + 2 * k, z, yh, core))
     for k in range(1, Z):
         greet(dev(l, z + k, yh, core))
-    pl.semaphore_wait(barrier, 11 + (NL // 2 - 1) + (Z - 1) + jnp.where(both, 2, 0))
+    pl.semaphore_wait(barrier, 2 * NL + 2 + (Z - 1) - jnp.where(both, 1, 0))
+
+    for cp in staged:
+        cp.wait()
 
     mine = pl.ds(pl.multiple_of(8 * l, 8), 8)
     here8 = pl.ds(pl.multiple_of(8 * l + 8, 8), 8)
-    quarter = 2 * yh + core
-    block_of = [(quarter + 1) % 4, (quarter + 3) % 4]
-    block = [jnp.where(core == 0, block_of[0], block_of[1]), jnp.where(core == 0, block_of[1], block_of[0])]
-
-    def holder(t, a, b):
-        return dev(flipped if t else l, z + b * (core + yh - 1), (yh + a) % 2, (core + b) % 2)
-
-    for n, (t, a, b) in enumerate(combos):
-        cp = remote(density, D.at[pl.ds(2 * block[b], 2), here8, :], s_d.at[n], r_d, holder(t, a, b))
-        cp.start()
-        pending.append(cp.wait_send)
-    pltpu.make_async_copy(density, D.at[pl.ds(2 * block[0], 2), here8, :], r_d).start()
-
-    def l_make(n, two):
-        a, b = ((1, 0), (0, 1), (1, 1))[n]
-        if two:
-            src, dst = labels, LAB.at[pl.ds(2 * block[b], 2)]
-        else:
-            src, dst = labels.at[core], LAB.at[2 * block[b] + core]
-        return remote(src, dst, s_l.at[n], r_l.at[block[b]], holder(a, a, b))
-
-    def l_each(act):
-        @pl.when(both)
+    two = pl.ds(2 * core + 2, 2)
+
+    def d_make(n, k):
+        return remote(density, D.at[two, here8, :], s_d.at[n, k], r_d, dev(l + n, z, k, yh))
+
+    def l_make(k):
+        return remote(labels, LAB.at[two], s_l.at[k], r_l.at[core], dev(l, z, k, yh))
+
+    def f_make(k):
+        return remote(forces.at[k], F.at[:, pl.ds(2 * core, 2)], s_f.at[k], r_f.at[core], dev(l, z, k, yh))
+
+    for n in far_first(NL)[:-1]:
+        for k in range(2):
+            cp = d_make(n, k)
+            cp.start()
+            pending.append(cp.wait_send)
+    for k in range(2):
+        @pl.when(is_self[k])
         def _():
-            act(l_make(0, True))
-
-        @pl.when(quarter == 1)
+            pltpu.make_async_copy(density, D.at[two, here8, :], r_d).start()
+            pltpu.make_async_copy(labels, LAB.at[two], r_l.at[core]).start()
+            pltpu.make_async_copy(forces.at[k], F.at[:, pl.ds(2 * core, 2)], r_f.at[core]).start()
+
+        @pl.when(jnp.logical_not(is_self[k]))
         def _():
-            act(l_make(0, False))
-
-        for n in (1, 2):
-            @pl.when(quarter == 0)
-            def _():
-                act(l_make(n, False))
-
-            @pl.when(quarter != 0)
-            def _():
-                act(l_make(n, True))
-
-    l_each(lambda cp: cp.start())
-    pending.append(lambda: l_each(lambda cp: cp.wait_send()))
-    pltpu.make_async_copy(labels, LAB.at[pl.ds(2 * block[0], 2)], r_l.at[block[0]]).start()
-
-    is_self = [jnp.logical_and(both, yh == 0), jnp.logical_and(both, yh == 1)]
-
-    def f_make(k):
-        return remote(
-            forces.at[k], F.at[:, pl.ds(2 * core, 2)], s_f.at[0, k], r_f.at[core], dev(l, z, k, yh)
-        )
-
-    def f_far(k):
-        return remote(
-            forces.at[k, :, yh], F.at[:, 4], s_f.at[1, k], r_f.at[2], dev(l, z + 2 * yh - 1, k, 1 - yh)
-        )
-
-    def f_sent():
+            d_make(0, k).start()
+            l_make(k).start()
+            f_make(k).start()
+
+    def native_sent():
         for k in range(2):
             @pl.when(jnp.logical_not(is_self[k]))
             def _():
+                d_make(0, k).wait_send()
+                l_make(k).wait_send()
                 f_make(k).wait_send()
 
-        @pl.when(both)
-        def _():
-            for k in range(2):
-                f_far(k).wait_send()
-
-    pending.append(f_sent)
-    get_weights = pltpu.make_async_copy(weights_in, weights, loc.at[0])
-    get_weights.start()
-
+    pending.append(native_sent)
     zero8 = jnp.zeros((8, 128), f32)
     for r in range(8):
         D[r, 0:8, :] = zero8
@@ -175,6 +160,7 @@
         V[r, rows + 8 : rows + 16, :] = zero8
         TX[r, 0:8, :] = zero8
         GU[r, 0:8, :] = zero8
+        GV[r, 0:8, :] = zero8
         for k in range(2):
             for c in range(3):
                 XA[k][c, r, rows : rows + 8, :] = zero8
@@ -186,53 +172,19 @@
         for k in range(2):
             MS[c, k, 2] = zero8
 
-    own16 = l // 2
-
-    def strip(x):
-        return D.at[:, pl.ds(pl.multiple_of(16 * x + 8, 8), 16), :]
-
-    arrived(strip(own16), r_d)
-    for k in range(1, NL // 2):
-        cp = remote(strip(own16), strip(own16), s_e.at[k - 1], r_e.at[k - 1], dev(l + 2 * k, z, yh, core))
+    arrived(D.at[2:6, 8 : rows + 8, :], r_d)
+    for k in range(2):
+        arrived(LAB.at[2 + 2 * k : 4 + 2 * k], r_l.at[k])
+
+    src2, dst2 = pl.ds(4 - 2 * core, 2), pl.ds(6 * core, 2)
+    got2 = pl.ds(6 * (1 - core), 2)
+    relays = [
+        remote(LAB.at[src2], LAB.at[pl.ds(6 * core, 2)], s_y.at[0], r_y.at[0], sibling),
+        remote(D.at[src2, 8 : rows + 8, :], D.at[dst2, 8 : rows + 8, :], s_y.at[1], r_y.at[1], sibling),
+    ]
+    for cp in relays:
         cp.start()
         pending.append(cp.wait_send)
-    for k in range(2):
-        @pl.when(is_self[k])
-        def _():
-            pltpu.make_async_copy(forces.at[k], F.at[:, pl.ds(2 * core, 2)], r_f.at[core]).start()
-
-        @pl.when(jnp.logical_not(is_self[k]))
-        def _():
-            f_make(k).start()
-
-    @pl.when(both)
-    def _():
-        for k in range(2):
-            f_far(k).start()
-
-    for k in range(1, NL // 2):
-        arrived(strip(lax.rem(own16 + NL // 2 - k, NL // 2)), r_e.at[k - 1])
-
-    @pl.when(jnp.logical_or(core == 0, yh == 0))
-    def _():
-        arrived(LAB.at[0:2], r_l.at[0])
-
-    @pl.when(quarter == 3)
-    def _():
-        arrived(LAB.at[1], r_l.at[0])
-
-    for b in (1, 2):
-        arrived(LAB.at[2 * b : 2 * b + 2], r_l.at[b])
-
-    @pl.when(core == 1)
-    def _():
-        arrived(LAB.at[6], r_l.at[3])
-
-    @pl.when(quarter == 2)
-    def _():
-        arrived(LAB.at[6:8], r_l.at[3])
-
-    sibling = dev(l, z, yh, 1 - core)
 
     sgn = 2 * core - 1
 
@@ -252,7 +204,37 @@
             TX[m, 8 * c + 8 : 8 * c + 16, :] = e + xprev(e)
         return 0
 
-    lax.fori_loop(0, 6, moduli_layer, 0)
+    lax.fori_loop(core, core + 4, moduli_layer, 0)
+
+    def e_make():
+        return remote(EM.at[4], EM.at[4], s_e, r_e, dev(l, far, yh, 1 - core))
+
+    @pl.when(core == 1)
+    def _():
+        e_make().start()
+
+    def e_sent():
+        @pl.when(core == 1)
+        def _():
+            e_make().wait_send()
+
+    pending.append(e_sent)
+
+    def w_make():
+        return remote(
+            D.at[pl.ds(2 + 2 * core, 2), 8 : rows + 8, :],
+            D.at[pl.ds(6 * (1 - core), 2), 8 : rows + 8, :],
+            s_w, r_w, dev(l, far, yh, 1 - core),
+        )
+
+    w_make().start()
+    pending.append(w_make().wait_send)
+    arrived(LAB.at[pl.ds(6 * (1 - core), 2)], r_y.at[0])
+    arrived(D.at[got2, 8 : rows + 8, :], r_y.at[1])
+
+    @pl.when(core == 1)
+    def _():
+        moduli_layer(0, 0)
 
     def inverse_layer(m, _):
         p = jnp.where(core == 1, 3 + m, 4 - m)
@@ -265,7 +247,22 @@
             INVD[m, 8 * c : 8 * c + 8, :] = jnp.where(lab != 1, (UNIT / DIAG) / (near + back), 0.0)
         return 0
 
-    lax.fori_loop(1, 6, inverse_layer, 0)
+    lax.fori_loop(1, 4, inverse_layer, 0)
+
+    @pl.when(core == 0)
+    def _():
+        arrived(EM.at[4], r_e)
+        known = jnp.where(inside(-1), f32(1.0), f32(0.0))
+        for c in range(NL):
+            e = EM[4, 8 * c : 8 * c + 8, :] * known
+            EM[4, 8 * c : 8 * c + 8, :] = e
+            TX[4, 8 * c + 8 : 8 * c + 16, :] = e + xprev(e)
+
+    inverse_layer(4, 0)
+
+    give_inverse = remote(INVD.at[4], INVD.at[5], s_i, r_i, dev(l, far, yh, 1 - core))
+    give_inverse.start()
+    pending.append(give_inverse.wait_send)
 
     def plane_sums(center, above, below):
         ysum = above + below
@@ -319,7 +316,8 @@
         return 0
 
     def filter_part(s):
-        if s == 1:
+        if s == 0:
+            arrived(D.at[pl.ds(6 * core, 2), 8 : rows + 8, :], r_w)
             lax.fori_loop(0, 8, d_plane, 0)
             lax.fori_loop(1, 7, v_plane, 0)
 
@@ -332,7 +330,6 @@
 
     for k in range(2):
         arrived(F.at[:, 2 * k : 2 * k + 2], r_f.at[k])
-    arrived(F.at[:, 4], r_f.at[2])
     flip = jnp.where(core == 1, f32(1.0), f32(-1.0))
 
     def x_make(par):
@@ -341,8 +338,11 @@
             for n, X in enumerate((XA, XD))
         ]
 
+    def z_make(n):
+        return remote(ZS.at[n], ZG.at[n], s_z.at[n], r_z.at[n], dev(l, far, yh, 1 - core))
+
     def first_step(m, _):
-        i = jnp.where(jnp.logical_or(core == 1, m == 5), m - 1, 4 - m)
+        i = jnp.where(core == 1, m - 1, 4 - m)
         for c in range(NL):
             at = slice(8 * c, 8 * c + 8)
             inv = INVD[m, at, :]
@@ -363,9 +363,17 @@
             for cp in x_make(0):
                 cp.start()
 
+        @pl.when(m == 4)
+        def _():
+            for comp in range(3):
+                for c in range(NL):
+                    ZS[0, comp, 8 * c : 8 * c + 8, :] = STEP[comp, 4, 8 * c : 8 * c + 8, :]
+            z_make(0).start()
+
         return 0
 
-    lax.fori_loop(1, 6, first_step, 0)
+    lax.fori_loop(1, 5, first_step, 0)
+    pending.append(z_make(0).wait_send)
 
     def fields(par, comp, m, c):
         a0 = XA[par][comp, m, 8 * c : 8 * c + 8, :]
@@ -395,19 +403,25 @@
 
     there = jnp.where(inside(jnp.where(core == 1, 8, -1)), f32(1.0), f32(0.0))
 
-    def z_make(par):
-        return remote(ZS.at[par], ZG.at[par], s_z.at[par], r_z.at[par], dev(l, far, yh, 1 - core))
-
-    def far_ghost(par):
-        arrived(ZG.at[par], r_z.at[par])
+    def far_ghost(s):
+        arrived(ZG.at[s], r_z.at[s])
+        par = s % 2
+        if s == 1:
+            arrived(INVD.at[5], r_i)
+            for c in range(NL):
+                INVD[5, 8 * c : 8 * c + 8, :] = INVD[5, 8 * c : 8 * c + 8, :] * there
         for comp in range(3):
             scale = -there if comp == 2 else there
             for c in range(NL):
                 at = slice(8 * c, 8 * c + 8)
-                v = ZG[par, comp, at, :] * scale
+                v = ZG[s, comp, at, :] * scale
+                if s > 0:
+                    v = v - coefs[s - 1][1] * (INVD[5, at, :] * KU[comp, at, :])
                 n = xnext(v)
                 XA[par][comp, 5, at, :] = v + n
                 XD[par][comp, 5, at, :] = n - v
+
+    coefs = chebyshev()
 
     def lay_out(half):
         for n in range(2):
@@ -423,8 +437,6 @@
         return remote(
             OUT.at[:, pl.ds(2 * half, 2)], disp.at[yh], s_o.at[half], r_o.at[yh], dev(l, z, core, half)
         )
-
-    coefs = chebyshev()
 
     def element_forces(par, m, c):
         u, v, w = modes(par, m, c)
@@ -459,6 +471,13 @@
         UP[4 * comp + 2, at, :] = gx + gzx
         UP[4 * comp + 3, at, :] = gxy + gxyz
 
+    def pull(buf, comp, c, taa, tay, tda, tdy):
+        buf[2 * comp, 8 * c + 8 : 8 * c + 16, :] = taa + tay
+        buf[2 * comp + 1, 8 * c + 8 : 8 * c + 16, :] = tda + tdy
+        a = (taa - tay) + buf[2 * comp, 8 * c + 7 : 8 * c + 15, :]
+        b = (tda - tdy) + buf[2 * comp + 1, 8 * c + 7 : 8 * c + 15, :]
+        return (a - b) + xprev(a + b)
+
     def sweep(s):
         par = s % 2
         nxt = 1 - par
@@ -469,16 +488,16 @@
             for comp, force in enumerate(element_forces(par, 0, c)):
                 push_up(comp, at, force)
 
+        def send_on(comp, m, at, step):
+            sent = SOL[comp, m, at, :] + step
+            SOL[comp, m, at, :] = sent
+            if s < SWEEPS - 1:
+                sent = step
+            n = xnext(sent)
+            XA[nxt][comp, m, at, :] = sent + n
+            XD[nxt][comp, m, at, :] = n - sent
+
         def layer(m, _):
-            if s > 0:
-                @pl.when(m == 4)
-                def _():
-                    if s == SWEEPS - 1:
-                        lay_out(1 - core)
-                        o_make(1 - core).start()
-                    filter_part(s)
-                    far_ghost(par)
-
             for c in range(NL):
                 at = slice(8 * c, 8 * c + 8)
                 inv = INVD[m, at, :]
@@ -489,22 +508,11 @@
                     tda = UP[4 * comp + 2, at, :] + (gx - gzx)
                     tdy = UP[4 * comp + 3, at, :] + (gxy - gxyz)
                     push_up(comp, at, force)
-                    GU[2 * comp, 8 * c + 8 : 8 * c + 16, :] = taa + tay
-                    GU[2 * comp + 1, 8 * c + 8 : 8 * c + 16, :] = tda + tdy
-                    a = (taa - tay) + GU[2 * comp, 8 * c + 7 : 8 * c + 15, :]
-                    b = (tda - tdy) + GU[2 * comp + 1, 8 * c + 7 : 8 * c + 15, :]
-                    pushed = (a - b) + xprev(a + b)
-                    res = R[comp, m, at, :] - pushed
+                    res = R[comp, m, at, :] - pull(GU, comp, c, taa, tay, tda, tdy)
                     R[comp, m, at, :] = res
                     step = c1 * STEP[comp, m, at, :] + c2 * (inv * res)
                     STEP[comp, m, at, :] = step
-                    sent = SOL[comp, m, at, :] + step
-                    SOL[comp, m, at, :] = sent
-                    if s < SWEEPS - 1:
-                        sent = step
-                    n = xnext(sent)
-                    XA[nxt][comp, m, at, :] = sent + n
-                    XD[nxt][comp, m, at, :] = n - sent
+                    send_on(comp, m, at, step)
 
             @pl.when(m == 1)
             def _():
@@ -513,24 +521,43 @@
                 for cp in x_make(nxt):
                     cp.start()
 
-            @pl.when(m == 4)
+            return 0
+
+        lax.fori_loop(1, 4, layer, 0)
+
+        for c in range(NL):
+            at = slice(8 * c, 8 * c + 8)
+            inv = INVD[4, at, :]
+            for comp in range(3):
+                held = [UP[4 * comp + f, at, :] for f in range(4)]
+                res = R[comp, 4, at, :] - pull(GU, comp, c, *held)
+                R[comp, 4, at, :] = res
+                step = c1 * STEP[comp, 4, at, :] + c2 * (inv * res)
+                STEP[comp, 4, at, :] = step
+                ZS[s + 1, comp, at, :] = SOL[comp, 4, at, :] + step if s == SWEEPS - 1 else step
+        if s < SWEEPS - 1:
+            z_make(s + 1).start()
+            pending.append(z_make(s + 1).wait_send)
+        else:
+            @pl.when(core == 0)
             def _():
-                if s > 0:
-                    z_make(par).wait_send()
-                for comp in range(3):
-                    for c in range(NL):
-                        at = slice(8 * c, 8 * c + 8)
-                        ZS[nxt, comp, at, :] = (STEP if s < SWEEPS - 1 else SOL)[comp, 4, at, :]
-                if s < SWEEPS - 1:
-                    z_make(nxt).start()
-                else:
-                    @pl.when(core == 0)
-                    def _():
-                        z_make(nxt).start()
-
-            return 0
-
-        lax.fori_loop(1, 5, layer, 0)
+                z_make(SWEEPS).start()
+
+            lay_out(1 - core)
+            o_make(1 - core).start()
+        filter_part(s)
+        far_ghost(s)
+        for c in range(NL):
+            at = slice(8 * c, 8 * c + 8)
+            inv = INVD[4, at, :]
+            for comp, force in enumerate(element_forces(par, 4, c)):
+                gz_, gy, gyz, gx, gzx, gxy, gxyz = force
+                near = pull(GU, comp, c, -gz_, gy - gyz, gx - gzx, gxy - gxyz)
+                KU[comp, at, :] = pull(GV, comp, c, gz_, gy + gyz, gx + gzx, gxy + gxyz)
+                R[comp, 4, at, :] = R[comp, 4, at, :] - near
+                step = STEP[comp, 4, at, :] - c2 * (inv * near)
+                STEP[comp, 4, at, :] = step
+                send_on(comp, 4, at, step)
 
     for s in range(SWEEPS):
         sweep(s)
@@ -558,14 +585,13 @@
     pending.append(o_ended)
 
     fin = SWEEPS % 2
-    get_weights.wait()
     pending.extend(cp.wait_send for cp in x_make(fin))
     pending.append(v_sent)
 
     def z_sent():
         @pl.when(core == 0)
         def _():
-            z_make(fin).wait_send()
+            z_make(SWEEPS).wait_send()
 
     pending.append(z_sent)
     weight = weights[2 * l + yh].astype(f32)
@@ -610,7 +636,7 @@
 
             @pl.when(core == 1)
             def _():
-                far_ghost(fin)
+                far_ghost(SWEEPS)
 
         return energy_layer(k, got)
 
@@ -626,7 +652,7 @@
         ll = lax.rem(l + k, NL)
         return remote(MS.at[ll, cc], RX.at[me], s_m.at[k, cc], r_m, dev(ll, z, core, cc))
 
-    for k in range(NL):
+    for k in far_first(NL):
         for cc in range(2):
             if k > 0:
                 m_make(k, cc).start()
@@ -655,20 +681,20 @@
 
     arrived(RX, r_m)
     scale = (3.0 * (1.0 - EMIN)) / weight_sum
-    sums = []
-    for k in range(3):
-        part = RX[0, k]
-        for n in range(1, 2 * NL):
-            part = part + RX[n, k]
-        sums.append(part)
-    rim = sums[2]
+    def summed(k):
+        parts = [RX[n, k] for n in range(2 * NL)]
+        while len(parts) > 1:
+            parts = [a + b for a, b in zip(parts[::2], parts[1::2])]
+        return parts[0]
+
+    rim = summed(2)
     SV[...] = rim[4:5, :]
 
     def s_make(kz, ky):
         return remote(SV, RX2.at[2 * z + yh], s_s.at[kz, ky], r_s, dev(l, z + kz, (yh + ky) % 2, core))
 
-    for kz in range(Z):
-        for ky in range(2):
+    for kz in far_first(Z):
+        for ky in (1, 0):
             if (kz, ky) != (0, 0):
                 s_make(kz, ky).start()
     pltpu.make_async_copy(SV, RX2.at[2 * z + yh], r_s).start()
@@ -682,7 +708,7 @@
     pending.append(s_sent)
     native = 4 * yh + 2 * (1 - core)
     for k in range(2):
-        main = sums[k]
+        main = summed(k)
         rated = []
         for n in range(3):
             near = pl.ds(pl.multiple_of(8 * l + 8 * n, 8), 8)
@@ -748,7 +774,10 @@
         vm = lambda *shape: pltpu.VMEM(shape, jnp.float32)
         dma = lambda *shape: pltpu.SemaphoreType.DMA(shape)
         scratch = [
-            vm(3, 5, rows, 128),
+            vm(*density.shape),
+            pltpu.VMEM(labels.shape, jnp.int32),
+            vm(*forces.shape),
+            vm(3, 4, rows, 128),
             pltpu.VMEM((8, rows, 128), jnp.int32),
             vm(8, rows + 16, 128),
             vm(6, rows, 128),
@@ -763,9 +792,11 @@
             vm(3, 6, rows + 8, 128),
             vm(12, rows, 128),
             vm(6, rows + 8, 128),
+            vm(6, rows + 8, 128),
+            vm(3, rows, 128),
             vm(3, 4, rows, 128),
-            vm(2, 3, rows, 128),
-            vm(2, 3, rows, 128),
+            vm(4, 3, rows, 128),
+            vm(4, 3, rows, 128),
             vm(8, rows, 128),
             vm(8, rows, 128),
             vm(6, rows + 16, 128),
@@ -778,18 +809,21 @@
             vm(2 * Z, 1, 128),
             pltpu.SMEM((2 * NL,), jnp.int32),
             vm(46 << 11, 128),
-            dma(7), pltpu.SemaphoreType.DMA,
-            dma(NL // 2), dma(NL // 2),
-            dma(2, 2), dma(3),
-            dma(3), dma(4),
+            dma(NL, 2), pltpu.SemaphoreType.DMA,
+            pltpu.SemaphoreType.DMA, pltpu.SemaphoreType.DMA,
+            dma(2), dma(2),
+            dma(2), dma(2),
+            dma(2), dma(2),
+            pltpu.SemaphoreType.DMA, pltpu.SemaphoreType.DMA,
+            pltpu.SemaphoreType.DMA, pltpu.SemaphoreType.DMA,
             pltpu.SemaphoreType.DMA, pltpu.SemaphoreType.DMA,
             dma(2, 2), dma(2, 2),
-            dma(2), dma(2),
+            dma(4), dma(4),
             dma(2), dma(2),
             dma(NL, 2), pltpu.SemaphoreType.DMA,
             dma(2), dma(2),
             dma(Z, 2), pltpu.SemaphoreType.DMA,
-            dma(1),
+            dma(4),
         ]
         return pl.pallas_call(
             functools.partial(kernel, NL, Z),

time: 49.5 us -> 45.6 us (0.921)
  Pallas kernels: 47.5 us -> 43.6 us
    pallas_call x1, Pallas kernels: 47.5 us -> 43.6 us  [on_device(): pl.pallas_call(functools.partial(kernel, NL, Z), out_shape=(pltpu.VMEM(de...]
where the time goes in v3:
time: 45.6 us; the launch traced here: 45.5 us
  Pallas kernels  43.6 us (96%)
  local copies, waits for them, and re-layouts  1.35 us (3%)
  between operations  0.64 us (1%)
    pallas_call x1, Pallas kernels, on_device(): pl.pallas_call(functools.partial(kernel, NL, Z), out_shape=(pltpu.VMEM(de...  43.6 us
    unnamed x2, local copies, waits for them, and re-layouts  1.35 us

profile of v3, /device:TPU:1, one launch (start us, length us, event | category | flops | bytes accessed | tf_op | source)
XLA Modules:
  0.0 45.5 jit_solution(10915855577512531075)
XLA Ops:
  0.6 43.6 %step.1 = (f32[2,8,128]{2,1,0:T(8,128)S(1)}, f32[2,3,2,64,128]{4,3,2,1,0:T(8,128)S(1)}) custom-call(f32[2,8,128]{2,1,0:T(8,128)} %density_in.1, s32[2,64,128]{2,1,0:T(8,128)} %labels_in.1, f32[2,3,2,64,128]{4,3,2,1,0:T(8,128)} %forces_in.1, s32[16]{0:T(128)} %weights_in.1), custom_call_target="tpu_custom_call" | custom-call | tf_op jit(solution)/shard_map/step/pallas_call | solution.py:828
  44.2 0.6 %copy.8 = f32[2,8,128]{2,1,0:T(8,128)} copy(f32[2,8,128]{2,1,0:T(8,128)S(1)} %get-tuple-element.2) | data formatting | bytes 16384
  44.8 0.7 %copy.9 = f32[2,3,2,64,128]{4,3,2,1,0:T(8,128)} copy(f32[2,3,2,64,128]{4,3,2,1,0:T(8,128)S(1)} %get-tuple-element.3) | data formatting | bytes 786432

commit v4 on v3

--- a/solution.py
+++ b/solution.py
@@ -341,7 +341,8 @@
     def z_make(n):
         return remote(ZS.at[n], ZG.at[n], s_z.at[n], r_z.at[n], dev(l, far, yh, 1 - core))
 
-    def first_step(m, _):
+    def first_step(n, _):
+        m = jnp.where(n == 0, 4, n)
         i = jnp.where(core == 1, m - 1, 4 - m)
         for c in range(NL):
             at = slice(8 * c, 8 * c + 8)
@@ -372,7 +373,7 @@
 
         return 0
 
-    lax.fori_loop(1, 5, first_step, 0)
+    lax.fori_loop(0, 4, first_step, 0)
     pending.append(z_make(0).wait_send)
 
     def fields(par, comp, m, c):
@@ -482,6 +483,25 @@
         par = s % 2
         nxt = 1 - par
         c1, c2 = coefs[s]
+
+        for c in range(NL):
+            at = slice(8 * c, 8 * c + 8)
+            inv = INVD[4, at, :]
+            for comp, force in enumerate(element_forces(par, 3, c)):
+                gz_, gy, gyz, gx, gzx, gxy, gxyz = force
+                res = R[comp, 4, at, :] - pull(GU, comp, c, gz_, gy + gyz, gx + gzx, gxy + gxyz)
+                R[comp, 4, at, :] = res
+                step = c1 * STEP[comp, 4, at, :] + c2 * (inv * res)
+                STEP[comp, 4, at, :] = step
+                ZS[s + 1, comp, at, :] = SOL[comp, 4, at, :] + step if s == SWEEPS - 1 else step
+        if s < SWEEPS - 1:
+            z_make(s + 1).start()
+            pending.append(z_make(s + 1).wait_send)
+        else:
+            @pl.when(core == 0)
+            def _():
+                z_make(SWEEPS).start()
+
         ghost(par)
         for c in range(NL):
             at = slice(8 * c, 8 * c + 8)
@@ -525,24 +545,7 @@
 
         lax.fori_loop(1, 4, layer, 0)
 
-        for c in range(NL):
-            at = slice(8 * c, 8 * c + 8)
-            inv = INVD[4, at, :]
-            for comp in range(3):
-                held = [UP[4 * comp + f, at, :] for f in range(4)]
-                res = R[comp, 4, at, :] - pull(GU, comp, c, *held)
-                R[comp, 4, at, :] = res
-                step = c1 * STEP[comp, 4, at, :] + c2 * (inv * res)
-                STEP[comp, 4, at, :] = step
-                ZS[s + 1, comp, at, :] = SOL[comp, 4, at, :] + step if s == SWEEPS - 1 else step
-        if s < SWEEPS - 1:
-            z_make(s + 1).start()
-            pending.append(z_make(s + 1).wait_send)
-        else:
-            @pl.when(core == 0)
-            def _():
-                z_make(SWEEPS).start()
-
+        if s == SWEEPS - 1:
             lay_out(1 - core)
             o_make(1 - core).start()
         filter_part(s)

time: 45.6 us -> 44.9 us (0.985)
  Pallas kernels: 43.6 us -> 42.8 us
    pallas_call x1, Pallas kernels: 43.6 us -> 42.8 us  [on_device(): pl.pallas_call(functools.partial(kernel, NL, Z), out_shape=(pltpu.VMEM(de...]
where the time goes in v4:
time: 44.9 us; the launch traced here: 44.8 us
  Pallas kernels  42.8 us (95%)
  local copies, waits for them, and re-layouts  1.35 us (3%)
  between operations  0.64 us (1%)
    pallas_call x1, Pallas kernels, on_device(): pl.pallas_call(functools.partial(kernel, NL, Z), out_shape=(pltpu.VMEM(de...  42.8 us
    unnamed x2, local copies, waits for them, and re-layouts  1.35 us

profile of v4, /device:TPU:1, one launch (start us, length us, event | category | flops | bytes accessed | tf_op | source)
XLA Modules:
  0.0 44.8 jit_solution(15193795822809849253)
XLA Ops:
  0.6 42.8 %step.1 = (f32[2,8,128]{2,1,0:T(8,128)S(1)}, f32[2,3,2,64,128]{4,3,2,1,0:T(8,128)S(1)}) custom-call(f32[2,8,128]{2,1,0:T(8,128)} %density_in.1, s32[2,64,128]{2,1,0:T(8,128)} %labels_in.1, f32[2,3,2,64,128]{4,3,2,1,0:T(8,128)} %forces_in.1, s32[16]{0:T(128)} %weights_in.1), custom_call_target="tpu_custom_call" | custom-call | tf_op jit(solution)/shard_map/step/pallas_call | solution.py:831
  43.4 0.6 %copy.8 = f32[2,8,128]{2,1,0:T(8,128)} copy(f32[2,8,128]{2,1,0:T(8,128)S(1)} %get-tuple-element.2) | data formatting | bytes 16384
  44.0 0.7 %copy.9 = f32[2,3,2,64,128]{4,3,2,1,0:T(8,128)} copy(f32[2,3,2,64,128]{4,3,2,1,0:T(8,128)S(1)} %get-tuple-element.3) | data formatting | bytes 786432

commit v5 on v4

--- a/solution.py
+++ b/solution.py
@@ -227,8 +227,6 @@
             s_w, r_w, dev(l, far, yh, 1 - core),
         )
 
-    w_make().start()
-    pending.append(w_make().wait_send)
     arrived(LAB.at[pl.ds(6 * (1 - core), 2)], r_y.at[0])
     arrived(D.at[got2, 8 : rows + 8, :], r_y.at[1])
 
@@ -262,6 +260,8 @@
 
     give_inverse = remote(INVD.at[4], INVD.at[5], s_i, r_i, dev(l, far, yh, 1 - core))
     give_inverse.start()
+    w_make().start()
+    pending.append(w_make().wait_send)
     pending.append(give_inverse.wait_send)
 
     def plane_sums(center, above, below):

time: 44.9 us -> 44.7 us (level)
  no operation moved by 1% of the time
where the time goes in v5:
time: 44.7 us; the launch traced here: 44.6 us
  Pallas kernels  42.6 us (95%)
  local copies, waits for them, and re-layouts  1.35 us (3%)
  between operations  0.64 us (1%)
    pallas_call x1, Pallas kernels, on_device(): pl.pallas_call(functools.partial(kernel, NL, Z), out_shape=(pltpu.VMEM(de...  42.6 us
    unnamed x2, local copies, waits for them, and re-layouts  1.35 us

profile of v5, /device:TPU:1, one launch (start us, length us, event | category | flops | bytes accessed | tf_op | source)
XLA Modules:
  0.0 44.6 jit_solution(15775548524892951103)
XLA Ops:
  0.6 42.6 %step.1 = (f32[2,8,128]{2,1,0:T(8,128)S(1)}, f32[2,3,2,64,128]{4,3,2,1,0:T(8,128)S(1)}) custom-call(f32[2,8,128]{2,1,0:T(8,128)} %density_in.1, s32[2,64,128]{2,1,0:T(8,128)} %labels_in.1, f32[2,3,2,64,128]{4,3,2,1,0:T(8,128)} %forces_in.1, s32[16]{0:T(128)} %weights_in.1), custom_call_target="tpu_custom_call" | custom-call | tf_op jit(solution)/shard_map/step/pallas_call | solution.py:831
  43.2 0.6 %copy.8 = f32[2,8,128]{2,1,0:T(8,128)} copy(f32[2,8,128]{2,1,0:T(8,128)S(1)} %get-tuple-element.2) | data formatting | bytes 16384
  43.8 0.7 %copy.9 = f32[2,3,2,64,128]{4,3,2,1,0:T(8,128)} copy(f32[2,3,2,64,128]{4,3,2,1,0:T(8,128)S(1)} %get-tuple-element.3) | data formatting | bytes 786432
